TPU v7x, 512 devices: a whole 4x4x16 slice. The times are simulated.
512 devices in a mesh: section: 4 (over x), dp: 32 (over z, core), tensor: 4 (over y).
Axes of the slice: x: 4, y: 4, z: 16, core: 2. Of those that a mesh axis runs over, the one named last changes fastest.
Arguments:
- text_embed: bfloat16 [8192, 3584], P('dp', 'tensor'), may hold values from -6 to 6
- vision: bfloat16 [2048, 2048], P('dp'), may hold values from -6 to 6
- proj_weight: bfloat16 [2048, 3584], P('dp', 'tensor'), may hold values from -0.125 to 0.125
- out_weight: bfloat16 [4, 3584, 3584], P('section', 'dp', 'tensor'), may hold values from -0.09375 to 0.09375
- qk_gain: float32 [4, 3584], P('section', 'tensor'), may hold values from 0.1 to 1.9
- image_counts: int32 [256], P('dp'), may hold values from 4 to 8, as said below
- sample_shard: int32 [256], P('dp'), may hold values from 0 to 31, as said below
- sample_offset: int32 [256], P('dp'), may hold values from 0 to 252, as said below
- embed_grad: bfloat16 [8192, 3584], P('dp', 'tensor'), may hold values from -6 to 6
Outputs:
- section_out: bfloat16 [4, 8192, 3584], P('section', 'dp', 'tensor')
- image_grad: bfloat16 [2048, 3584], P('dp', 'tensor')
Inputs may be any that keep to these rules, and one draw needn't show every extreme that they name: `image_counts`: every encoder device has a sample with exactly 8 image rows and one with exactly 4. `sample_shard`: each dp index receives exactly 8 samples; a dp index that sends samples to another sends it exactly 1. `sample_offset`: A sample's image rows lie inside one document of its shard, and each document of a shard holds the image rows of exactly one sample.
All inputs are finite; a program needn't handle non-finite values.
Results may differ from a plain program's by a relative error of at most 0.0095.
Values may be sent and summed in bfloat16 or wider, within the bound.
A program may use at most 64 MiB of HBM per device.

v0:
```python
import jax
import jax.numpy as jnp
from jax import lax
from jax.sharding import PartitionSpec as P

HEAD = 128
DOC = 32
SLOT = 8
MICRO = 8


def from_behind(shard, axis, by):
    length = lax.axis_size(axis)
    pairs = [(i, i + by) for i in range(length) if 0 <= i + by < length]
    return lax.ppermute(shard, axis, pairs)


def attend(block, gains):
    rows, width = block.shape
    heads = width // HEAD
    values = block.reshape(rows // DOC, DOC, heads, HEAD)
    widened = values.astype(jnp.float32)
    square_mean = jnp.mean(widened * widened, axis=-1, keepdims=True)
    normed = widened * lax.rsqrt(square_mean + 1e-06) * gains.reshape(heads, HEAD)
    scores = jnp.einsum("dqhe,dkhe->dhqk", normed, normed, precision=lax.Precision.HIGHEST) * (
        2.0 / HEAD
    )
    query_pos = lax.broadcasted_iota(jnp.int32, (DOC, DOC), 0)
    key_pos = lax.broadcasted_iota(jnp.int32, (DOC, DOC), 1)
    weights = jnp.where(key_pos <= query_pos, jnp.exp(scores), 0.0)
    weights = (weights / jnp.sum(weights, axis=-1, keepdims=True)).astype(jnp.bfloat16)
    mixed = jnp.einsum("dhqk,dkhe->dqhe", weights, values, preferred_element_type=jnp.float32)
    return mixed.reshape(rows, width).astype(jnp.bfloat16)


def on_device(
    text_embed,
    vision,
    proj_weight,
    out_weight,
    qk_gain,
    image_counts,
    sample_shard,
    sample_offset,
    embed_grad,
):
    out_full, proj_full = (
        lax.all_gather(out_weight[0], "dp", axis=0, tiled=True),
        lax.all_gather(proj_weight, "dp", axis=0, tiled=True),
    )
    gains = qk_gain[0]
    dp_devices = lax.axis_size("dp")
    samples = sample_shard.shape[0]
    pairs = max(1, samples // dp_devices)
    slots = dp_devices * pairs
    width = text_embed.shape[1]
    feature_count = vision.shape[1]
    later = lax.broadcasted_iota(jnp.int32, (samples, samples), 0)
    former = lax.broadcasted_iota(jnp.int32, (samples, samples), 1)
    same_dest = (sample_shard[:, None] == sample_shard[None, :]) & (former < later)
    rank_within = jnp.sum(same_dest.astype(jnp.int32), axis=1)
    slot_index = sample_shard * pairs + rank_within
    select = slot_index[None, :] == lax.broadcasted_iota(jnp.int32, (slots, samples), 0)
    select_mat = select.astype(jnp.bfloat16)
    details = jnp.stack([sample_offset, image_counts], axis=1)
    slot_details = jnp.sum(jnp.where(select[:, :, None], details[None, :, :], 0), axis=1)
    slot_details = slot_details.reshape(dp_devices, pairs, 2)
    raw_rows = vision.reshape(samples, SLOT * feature_count)
    outgoing = jnp.dot(select_mat, raw_rows, preferred_element_type=jnp.float32).astype(
        jnp.bfloat16
    )
    outgoing = outgoing.reshape(dp_devices, pairs * SLOT, feature_count)
    arrived, arrived_details = (
        lax.all_to_all(outgoing, "dp", split_axis=0, concat_axis=0, tiled=True),
        lax.all_to_all(slot_details, "dp", split_axis=0, concat_axis=0, tiled=True),
    )
    flat_rows = arrived.reshape(slots * SLOT, feature_count)
    image_slots = jnp.dot(flat_rows, proj_full, preferred_element_type=jnp.float32).astype(
        jnp.bfloat16
    )
    arrived_details = arrived_details.reshape(slots, 2)
    within = lax.broadcasted_iota(jnp.int32, (slots, SLOT), 1)
    target = jnp.where(
        within < arrived_details[:, 1:2], arrived_details[:, 0:1] + within, -1
    ).reshape(slots * SLOT)
    shard_rows = text_embed.shape[0]
    placing = target[None, :] == lax.broadcasted_iota(jnp.int32, (shard_rows, slots * SLOT), 0)
    placing_mat = placing.astype(jnp.bfloat16)
    image_rows = jnp.dot(placing_mat, image_slots, preferred_element_type=jnp.float32).astype(
        jnp.bfloat16
    )
    embedded = jnp.where(jnp.any(placing, axis=1)[:, None], image_rows, text_embed)
    returned = jnp.dot(placing_mat.T, embed_grad, preferred_element_type=jnp.float32).astype(
        jnp.bfloat16
    )
    returned = lax.all_to_all(
        returned.reshape(dp_devices, pairs * SLOT, width),
        "dp",
        split_axis=0,
        concat_axis=0,
        tiled=True,
    )
    gathered_back = jnp.dot(
        select_mat.T, returned.reshape(slots, SLOT * width), preferred_element_type=jnp.float32
    )
    image_grad = gathered_back.astype(jnp.bfloat16).reshape(samples * SLOT, width)
    section_index = lax.axis_index("section")
    section_count = lax.axis_size("section")
    micro_rows = shard_rows // MICRO
    incoming = jnp.zeros((micro_rows, width), jnp.bfloat16)
    outputs = jnp.zeros((shard_rows, width), jnp.bfloat16)
    step_count = MICRO + section_count - 1
    for step in range(step_count):
        lower = min(step, MICRO - 1) * micro_rows
        first_rows = embedded[lower : lower + micro_rows]
        block = jnp.where(section_index == 0, first_rows, incoming)
        mixed = attend(block, gains)
        total = block.astype(jnp.float32) + jnp.dot(
            lax.all_gather(mixed, "tensor", axis=1, tiled=True),
            out_full,
            preferred_element_type=jnp.float32,
        )
        result = total.astype(jnp.bfloat16)
        micro_index = step - section_index
        active = (micro_index >= 0) & (micro_index < MICRO)
        place_at = jnp.clip(micro_index, 0, MICRO - 1) * micro_rows
        current = lax.dynamic_slice_in_dim(outputs, place_at, micro_rows, 0)
        outputs = lax.dynamic_update_slice_in_dim(
            outputs, jnp.where(active, result, current), place_at, 0
        )
        if step + 1 < step_count:
            incoming = from_behind(result, "section", 1)
    return (outputs[None], image_grad)


def solution(mesh):
    placed = (
        P("dp", "tensor"),
        P("dp", None),
        P("dp", "tensor"),
        P("section", "dp", "tensor"),
        P("section", "tensor"),
        P("dp"),
        P("dp"),
        P("dp"),
        P("dp", "tensor"),
    )
    return jax.shard_map(
        on_device,
        mesh=mesh,
        in_specs=placed,
        out_specs=(P("section", "dp", "tensor"), P("dp", "tensor")),
        check_vma=False,
    )
```

profile of v0, /device:TPU:6, one launch (start us, length us, event | category | flops | bytes accessed | tf_op | source)
XLA Modules:
  0.0 440.6 jit_solution(13636320920249505000)
XLA Ops:
  11.8 15.5 %all-to-all-start = ((s32[32,1,2]{2,1,0:T(1,128)}), s32[32,1,2]{2,1,0:T(1,128)S(1)}, u32[]{:S(2)}, u32[]{:S(2)}) async-start(s32[32,1,2]{2,1,0:T(1,128)} %copy.159), calls=%async_computation | async-start | bytes 32768 | tf_op jit(solution)/shard_map/all_to_all | solution.py:75
  28.9 1.6 copy.238
  30.5 9.2 %all-to-all-done = s32[32,1,2]{2,1,0:T(1,128)S(1)} async-done(((s32[32,1,2]{2,1,0:T(1,128)}), s32[32,1,2]{2,1,0:T(1,128)S(1)}, u32[]{:S(2)}, u32[]{:S(2)}) %all-to-all-start) | async-done | bytes 288 | tf_op jit(solution)/shard_map/all_to_all | solution.py:75
  39.7 3.9 all-to-all-start.1
  44.1 65.3 %all-to-all-done.1 = bf16[32,8,2048]{2,1,0:T(8,128)(2,1)S(1)} async-done(((bf16[32,8,2048]{2,1,0:T(8,128)(2,1)}), bf16[32,8,2048]{2,1,0:T(8,128)(2,1)S(1)}, u32[]{:S(2)}, u32[]{:S(2)}) %all-to-all-start.1) | async-done | bytes 1048608 | tf_op jit(solution)/shard_map/all_to_all | solution.py:74
  109.3 4.3 all-gather.4.cloned.1.call-done
  113.6 3.5 fusion.23
  118.1 12.8 %all_gather.40 = bf16[32,3584]{1,0:T(8,128)(2,1)S(1)} all-gather(bf16[32,896]{1,0:T(8,128)(2,1)S(1)} %bitcast.345), channel_id=1, replica_groups=mesh['section'=4,'dp'=32,'tensor'=4] {'tensor'}, dimensions={1}, use_global_device_ids=true | all-gather | bytes 286720 | tf_op jit(solution)/shard_map/all_gather | solution.py:119
  130.9 59.5 %all-gather.6.cloned.1.call-done = bf16[1,3584,896]{2,1,0:T(8,128)(2,1)} async-done(((bf16[1,112,896]{2,1,0:T(8,128)(2,1)}), bf16[1,3584,896]{2,1,0:T(8,128)(2,1)}) %all-gather.6.cloned.1.call-update) | async-done | bytes 6422544 | tf_op jit(solution)/shard_map/all_gather | solution.py:48
  190.4 4.0 select_dynamic-update-slice_fusion.9
  194.4 1.3 collective-permute-start
  195.7 4.8 %collective-permute-done = bf16[32,896]{1,0:T(8,128)(2,1)S(1)} collective-permute-done((bf16[32,896]{1,0:T(8,128)(2,1)S(1)}, bf16[32,896]{1,0:T(8,128)(2,1)S(1)}, u32[]{:S(2)}, u32[]{:S(2)}) %collective-permute-start) | collective-permute-done | bytes 57376 | tf_op jit(solution)/shard_map/ppermute | solution.py:15
  201.5 12.6 %all_gather.42 = bf16[32,3584]{1,0:T(8,128)(2,1)S(1)} all-gather(bf16[32,896]{1,0:T(8,128)(2,1)S(1)} %bitcast.346), channel_id=1, replica_groups=mesh['section'=4,'dp'=32,'tensor'=4] {'tensor'}, dimensions={1}, use_global_device_ids=true | all-gather | bytes 286720 | tf_op jit(solution)/shard_map/all_gather | solution.py:119
  214.0 4.0 select_dynamic-update-slice_fusion.8
  218.1 1.3 collective-permute-start.1
  219.4 4.8 %collective-permute-done.1 = bf16[32,896]{1,0:T(8,128)(2,1)S(1)} collective-permute-done((bf16[32,896]{1,0:T(8,128)(2,1)S(1)}, bf16[32,896]{1,0:T(8,128)(2,1)S(1)}, u32[]{:S(2)}, u32[]{:S(2)}) %collective-permute-start.1) | collective-permute-done | bytes 57376 | tf_op jit(solution)/shard_map/ppermute | solution.py:15
  225.1 12.2 %all_gather.43 = bf16[32,3584]{1,0:T(8,128)(2,1)S(1)} all-gather(bf16[32,896]{1,0:T(8,128)(2,1)S(1)} %bitcast.347), channel_id=1, replica_groups=mesh['section'=4,'dp'=32,'tensor'=4] {'tensor'}, dimensions={1}, use_global_device_ids=true | all-gather | bytes 286720 | tf_op jit(solution)/shard_map/all_gather | solution.py:119
  237.4 4.0 select_dynamic-update-slice_fusion.7
  241.4 1.3 collective-permute-start.2
  242.7 4.8 %collective-permute-done.2 = bf16[32,896]{1,0:T(8,128)(2,1)S(1)} collective-permute-done((bf16[32,896]{1,0:T(8,128)(2,1)S(1)}, bf16[32,896]{1,0:T(8,128)(2,1)S(1)}, u32[]{:S(2)}, u32[]{:S(2)}) %collective-permute-start.2) | collective-permute-done | bytes 57376 | tf_op jit(solution)/shard_map/ppermute | solution.py:15
  248.4 12.2 %all_gather.44 = bf16[32,3584]{1,0:T(8,128)(2,1)S(1)} all-gather(bf16[32,896]{1,0:T(8,128)(2,1)S(1)} %bitcast.348), channel_id=1, replica_groups=mesh['section'=4,'dp'=32,'tensor'=4] {'tensor'}, dimensions={1}, use_global_device_ids=true | all-gather | bytes 286720 | tf_op jit(solution)/shard_map/all_gather | solution.py:119
  260.7 4.0 select_dynamic-update-slice_fusion.6
  264.7 1.3 collective-permute-start.3
  266.0 4.8 %collective-permute-done.3 = bf16[32,896]{1,0:T(8,128)(2,1)S(1)} collective-permute-done((bf16[32,896]{1,0:T(8,128)(2,1)S(1)}, bf16[32,896]{1,0:T(8,128)(2,1)S(1)}, u32[]{:S(2)}, u32[]{:S(2)}) %collective-permute-start.3) | collective-permute-done | bytes 57376 | tf_op jit(solution)/shard_map/ppermute | solution.py:15
  271.7 12.4 %all_gather.45 = bf16[32,3584]{1,0:T(8,128)(2,1)S(1)} all-gather(bf16[32,896]{1,0:T(8,128)(2,1)S(1)} %bitcast.349), channel_id=1, replica_groups=mesh['section'=4,'dp'=32,'tensor'=4] {'tensor'}, dimensions={1}, use_global_device_ids=true | all-gather | bytes 286720 | tf_op jit(solution)/shard_map/all_gather | solution.py:119
  284.1 4.0 select_dynamic-update-slice_fusion.5
  288.1 1.3 collective-permute-start.4
  289.4 4.8 %collective-permute-done.4 = bf16[32,896]{1,0:T(8,128)(2,1)S(1)} collective-permute-done((bf16[32,896]{1,0:T(8,128)(2,1)S(1)}, bf16[32,896]{1,0:T(8,128)(2,1)S(1)}, u32[]{:S(2)}, u32[]{:S(2)}) %collective-permute-start.4) | collective-permute-done | bytes 57376 | tf_op jit(solution)/shard_map/ppermute | solution.py:15
  295.2 12.5 %all_gather.46 = bf16[32,3584]{1,0:T(8,128)(2,1)S(1)} all-gather(bf16[32,896]{1,0:T(8,128)(2,1)S(1)} %bitcast.350), channel_id=1, replica_groups=mesh['section'=4,'dp'=32,'tensor'=4] {'tensor'}, dimensions={1}, use_global_device_ids=true | all-gather | bytes 286720 | tf_op jit(solution)/shard_map/all_gather | solution.py:119
  307.7 4.0 select_dynamic-update-slice_fusion.4
  311.7 1.3 collective-permute-start.5
  313.0 4.8 %collective-permute-done.5 = bf16[32,896]{1,0:T(8,128)(2,1)S(1)} collective-permute-done((bf16[32,896]{1,0:T(8,128)(2,1)S(1)}, bf16[32,896]{1,0:T(8,128)(2,1)S(1)}, u32[]{:S(2)}, u32[]{:S(2)}) %collective-permute-start.5) | collective-permute-done | bytes 57376 | tf_op jit(solution)/shard_map/ppermute | solution.py:15
  318.7 12.2 %all_gather.47 = bf16[32,3584]{1,0:T(8,128)(2,1)S(1)} all-gather(bf16[32,896]{1,0:T(8,128)(2,1)S(1)} %bitcast.351), channel_id=1, replica_groups=mesh['section'=4,'dp'=32,'tensor'=4] {'tensor'}, dimensions={1}, use_global_device_ids=true | all-gather | bytes 286720 | tf_op jit(solution)/shard_map/all_gather | solution.py:119
  331.0 4.0 select_dynamic-update-slice_fusion.3
  337.4 7.9 %all-to-all-start.2 = ((bf16[32,8,896]{2,1,0:T(8,128)(2,1)}), bf16[32,8,896]{2,1,0:T(8,128)(2,1)S(1)}, u32[]{:S(2)}, u32[]{:S(2)}) async-start(bf16[32,8,896]{2,1,0:T(8,128)(2,1)} %fusion.22), calls=%async_computation.2 | async-start | bytes 917504 | tf_op jit(solution)/shard_map/all_to_all | solution.py:96
  346.2 12.2 %all_gather.48 = bf16[32,3584]{1,0:T(8,128)(2,1)S(1)} all-gather(bf16[32,896]{1,0:T(8,128)(2,1)S(1)} %bitcast.352), channel_id=1, replica_groups=mesh['section'=4,'dp'=32,'tensor'=4] {'tensor'}, dimensions={1}, use_global_device_ids=true | all-gather | bytes 286720 | tf_op jit(solution)/shard_map/all_gather | solution.py:119
  358.5 4.0 select_dynamic-update-slice_fusion.2
  362.5 1.3 collective-permute-start.7
  363.8 5.4 %collective-permute-done.7 = bf16[32,896]{1,0:T(8,128)(2,1)S(1)} collective-permute-done((bf16[32,896]{1,0:T(8,128)(2,1)S(1)}, bf16[32,896]{1,0:T(8,128)(2,1)S(1)}, u32[]{:S(2)}, u32[]{:S(2)}) %collective-permute-start.7) | collective-permute-done | bytes 57376 | tf_op jit(solution)/shard_map/ppermute | solution.py:15
  370.2 12.2 %all_gather.49 = bf16[32,3584]{1,0:T(8,128)(2,1)S(1)} all-gather(bf16[32,896]{1,0:T(8,128)(2,1)S(1)} %bitcast.353), channel_id=1, replica_groups=mesh['section'=4,'dp'=32,'tensor'=4] {'tensor'}, dimensions={1}, use_global_device_ids=true | all-gather | bytes 286720 | tf_op jit(solution)/shard_map/all_gather | solution.py:119
  382.4 4.0 select_dynamic-update-slice_fusion.1
  387.8 4.7 %collective-permute-done.8 = bf16[32,896]{1,0:T(8,128)(2,1)S(1)} collective-permute-done((bf16[32,896]{1,0:T(8,128)(2,1)S(1)}, bf16[32,896]{1,0:T(8,128)(2,1)S(1)}, u32[]{:S(2)}, u32[]{:S(2)}) %collective-permute-start.8) | collective-permute-done | bytes 57376 | tf_op jit(solution)/shard_map/ppermute | solution.py:15
  393.5 12.2 %all_gather.50 = bf16[32,3584]{1,0:T(8,128)(2,1)S(1)} all-gather(bf16[32,896]{1,0:T(8,128)(2,1)S(1)} %bitcast.354), channel_id=1, replica_groups=mesh['section'=4,'dp'=32,'tensor'=4] {'tensor'}, dimensions={1}, use_global_device_ids=true | all-gather | bytes 286720 | tf_op jit(solution)/shard_map/all_gather | solution.py:119
  405.7 4.0 select_dynamic-update-slice_fusion
  409.7 1.3 collective-permute-start.9
  412.0 3.8 collective-permute-done.9
  416.8 12.2 %all_gather.51 = bf16[32,3584]{1,0:T(8,128)(2,1)S(1)} all-gather(bf16[32,896]{1,0:T(8,128)(2,1)S(1)} %bitcast.355), channel_id=1, replica_groups=mesh['section'=4,'dp'=32,'tensor'=4] {'tensor'}, dimensions={1}, use_global_device_ids=true | all-gather | bytes 286720 | tf_op jit(solution)/shard_map/all_gather | solution.py:119
  429.0 4.0 fusion.129
  (147 shorter events, 22.2 us)
Async XLA Ops:
  7.2 329.1 %copy-start = (bf16[256,896]{1,0:T(8,128)(2,1)S(1)}, bf16[256,896]{1,0:T(8,128)(2,1)}, u32[]{:S(2)}) copy-start(bf16[256,896]{1,0:T(8,128)(2,1)} %param.17) | copy-start | bytes 1376260
  7.2 36.4 %copy-start.2 = (f32[1,896]{1,0:T(1,128)S(1)}, f32[1,896]{1,0:T(1,128)}, u32[]{:S(2)}) copy-start(f32[1,896]{1,0:T(1,128)} %param.13) | copy-start | bytes 10756
  7.2 106.5 %copy-start.3 = (bf16[256,896]{1,0:T(8,128)(2,1)S(1)}, bf16[256,896]{1,0:T(8,128)(2,1)}, u32[]{:S(2)}) copy-start(bf16[256,896]{1,0:T(8,128)(2,1)} %param.9) | copy-start | bytes 1376260
  7.2 106.4 %all-gather.4.cloned.1.call-start = ((), (), s32[]{:S(2)}) async-start(), calls=%async_computation.3 | async-start | bytes 3784704 | tf_op jit(solution)/shard_map/all_gather | solution.py:49
  7.9 182.5 %all-gather.6.cloned.1.call-start = ((), (), s32[]{:S(2)}) async-start(), calls=%async_computation.4 | async-start | bytes 6623232 | tf_op jit(solution)/shard_map/all_gather | solution.py:48
  11.8 27.9 %all-to-all-start = ((s32[32,1,2]{2,1,0:T(1,128)}), s32[32,1,2]{2,1,0:T(1,128)S(1)}, u32[]{:S(2)}, u32[]{:S(2)}) async-start(s32[32,1,2]{2,1,0:T(1,128)} %copy.159), calls=%async_computation | async-start | bytes 32768 | tf_op jit(solution)/shard_map/all_to_all | solution.py:75
  39.7 69.7 %all-to-all-start.1 = ((bf16[32,8,2048]{2,1,0:T(8,128)(2,1)}), bf16[32,8,2048]{2,1,0:T(8,128)(2,1)S(1)}, u32[]{:S(2)}, u32[]{:S(2)}) async-start(bf16[32,8,2048]{2,1,0:T(8,128)(2,1)} %bitcast.68), calls=%async_computation.1 | async-start | bytes 2097152 | tf_op jit(solution)/shard_map/all_to_all | solution.py:74
  194.4 6.1 %collective-permute-start = (bf16[32,896]{1,0:T(8,128)(2,1)S(1)}, bf16[32,896]{1,0:T(8,128)(2,1)S(1)}, u32[]{:S(2)}, u32[]{:S(2)}) collective-permute-start(bf16[32,896]{1,0:T(8,128)(2,1)S(1)} %get-tuple-element.27), channel_id=1, source_target_pairs={{0,128},{128,256},{256,384},{1,129},{129,257},{257,385},{2,130},{1... | collective-permute-start | bytes 172040 | tf_op jit(solution)/shard_map/ppermute | solution.py:15
  218.1 6.1 %collective-permute-start.1 = (bf16[32,896]{1,0:T(8,128)(2,1)S(1)}, bf16[32,896]{1,0:T(8,128)(2,1)S(1)}, u32[]{:S(2)}, u32[]{:S(2)}) collective-permute-start(bf16[32,896]{1,0:T(8,128)(2,1)S(1)} %get-tuple-element.29), channel_id=1, source_target_pairs={{0,128},{128,256},{256,384},{1,129},{129,257},{257,385},{2,130},{1... | collective-permute-start | bytes 172040 | tf_op jit(solution)/shard_map/ppermute | solution.py:15
  241.4 6.1 %collective-permute-start.2 = (bf16[32,896]{1,0:T(8,128)(2,1)S(1)}, bf16[32,896]{1,0:T(8,128)(2,1)S(1)}, u32[]{:S(2)}, u32[]{:S(2)}) collective-permute-start(bf16[32,896]{1,0:T(8,128)(2,1)S(1)} %get-tuple-element.31), channel_id=1, source_target_pairs={{0,128},{128,256},{256,384},{1,129},{129,257},{257,385},{2,130},{1... | collective-permute-start | bytes 172040 | tf_op jit(solution)/shard_map/ppermute | solution.py:15
  264.7 6.1 %collective-permute-start.3 = (bf16[32,896]{1,0:T(8,128)(2,1)S(1)}, bf16[32,896]{1,0:T(8,128)(2,1)S(1)}, u32[]{:S(2)}, u32[]{:S(2)}) collective-permute-start(bf16[32,896]{1,0:T(8,128)(2,1)S(1)} %get-tuple-element.33), channel_id=1, source_target_pairs={{0,128},{128,256},{256,384},{1,129},{129,257},{257,385},{2,130},{1... | collective-permute-start | bytes 172040 | tf_op jit(solution)/shard_map/ppermute | solution.py:15
  288.1 6.1 %collective-permute-start.4 = (bf16[32,896]{1,0:T(8,128)(2,1)S(1)}, bf16[32,896]{1,0:T(8,128)(2,1)S(1)}, u32[]{:S(2)}, u32[]{:S(2)}) collective-permute-start(bf16[32,896]{1,0:T(8,128)(2,1)S(1)} %get-tuple-element.35), channel_id=1, source_target_pairs={{0,128},{128,256},{256,384},{1,129},{129,257},{257,385},{2,130},{1... | collective-permute-start | bytes 172040 | tf_op jit(solution)/shard_map/ppermute | solution.py:15
  311.7 6.1 %collective-permute-start.5 = (bf16[32,896]{1,0:T(8,128)(2,1)S(1)}, bf16[32,896]{1,0:T(8,128)(2,1)S(1)}, u32[]{:S(2)}, u32[]{:S(2)}) collective-permute-start(bf16[32,896]{1,0:T(8,128)(2,1)S(1)} %get-tuple-element.37), channel_id=1, source_target_pairs={{0,128},{128,256},{256,384},{1,129},{129,257},{257,385},{2,130},{1... | collective-permute-start | bytes 172040 | tf_op jit(solution)/shard_map/ppermute | solution.py:15
  334.9 10.3 %collective-permute-start.6 = (bf16[32,896]{1,0:T(8,128)(2,1)S(1)}, bf16[32,896]{1,0:T(8,128)(2,1)S(1)}, u32[]{:S(2)}, u32[]{:S(2)}) collective-permute-start(bf16[32,896]{1,0:T(8,128)(2,1)S(1)} %get-tuple-element.39), channel_id=1, source_target_pairs={{0,128},{128,256},{256,384},{1,129},{129,257},{257,385},{2,130},{1... | collective-permute-start | bytes 172040 | tf_op jit(solution)/shard_map/ppermute | solution.py:15
  337.4 50.4 %all-to-all-start.2 = ((bf16[32,8,896]{2,1,0:T(8,128)(2,1)}), bf16[32,8,896]{2,1,0:T(8,128)(2,1)S(1)}, u32[]{:S(2)}, u32[]{:S(2)}) async-start(bf16[32,8,896]{2,1,0:T(8,128)(2,1)} %fusion.22), calls=%async_computation.2 | async-start | bytes 917504 | tf_op jit(solution)/shard_map/all_to_all | solution.py:96
  362.5 6.7 %collective-permute-start.7 = (bf16[32,896]{1,0:T(8,128)(2,1)S(1)}, bf16[32,896]{1,0:T(8,128)(2,1)S(1)}, u32[]{:S(2)}, u32[]{:S(2)}) collective-permute-start(bf16[32,896]{1,0:T(8,128)(2,1)S(1)} %get-tuple-element.41), channel_id=1, source_target_pairs={{0,128},{128,256},{256,384},{1,129},{129,257},{257,385},{2,130},{1... | collective-permute-start | bytes 172040 | tf_op jit(solution)/shard_map/ppermute | solution.py:15
  386.4 6.1 %collective-permute-start.8 = (bf16[32,896]{1,0:T(8,128)(2,1)S(1)}, bf16[32,896]{1,0:T(8,128)(2,1)S(1)}, u32[]{:S(2)}, u32[]{:S(2)}) collective-permute-start(bf16[32,896]{1,0:T(8,128)(2,1)S(1)} %get-tuple-element.43), channel_id=1, source_target_pairs={{0,128},{128,256},{256,384},{1,129},{129,257},{257,385},{2,130},{1... | collective-permute-start | bytes 172040 | tf_op jit(solution)/shard_map/ppermute | solution.py:15
  409.7 6.1 %collective-permute-start.9 = (bf16[32,896]{1,0:T(8,128)(2,1)S(1)}, bf16[32,896]{1,0:T(8,128)(2,1)S(1)}, u32[]{:S(2)}, u32[]{:S(2)}) collective-permute-start(bf16[32,896]{1,0:T(8,128)(2,1)S(1)} %get-tuple-element.45), channel_id=1, source_target_pairs={{0,128},{128,256},{256,384},{1,129},{129,257},{257,385},{2,130},{1... | collective-permute-start | bytes 172040 | tf_op jit(solution)/shard_map/ppermute | solution.py:15
  433.0 0.8 copy-start.1
Sparse Core Ops, SparseCore 0:
  10.2 103.4 all-gather.3
  115.8 74.5 all-gather.5
where the time goes:
time: 443 us; the launch traced here: 441 us
  waiting for transfers between devices  182 us (41%)
  blocking collectives  136 us (31%)
  matrix products  55.1 us (12%)
  starting transfers between devices  40.3 us (9%)
  between operations  15.2 us (3%)
  local copies, waits for them, and re-layouts  6.79 us (2%)
  other arithmetic  5.23 us (1%)
    all_gather x11, blocking collectives, on_device(): lax.all_gather(mixed, 'tensor', axis=1, tiled=True)  136 us
    all_to_all x1, waiting for transfers between devices, on_device(): lax.all_to_all(outgoing, 'dp', split_axis=0, concat_axis=0, tiled=True)  65.3 us
    all_gather x1, waiting for transfers between devices, on_device(): lax.all_gather(out_weight[0], 'dp', axis=0, tiled=True)  59.5 us
    dot_general x11, matrix products, on_device(): jnp.dot(lax.all_gather(mixed, 'tensor', axis=1, tiled=True), out_full, pr...  43.9 us
    ppermute x10, waiting for transfers between devices, from_behind(): return lax.ppermute(shard, axis, pairs)  42.5 us
    all_to_all x1, starting transfers between devices, on_device(): lax.all_to_all(slot_details, 'dp', split_axis=0, concat_axis=0, tiled=True)  15.5 us
    ppermute x10, starting transfers between devices, from_behind(): return lax.ppermute(shard, axis, pairs)  12.9 us
    all_to_all x1, waiting for transfers between devices, on_device(): lax.all_to_all(slot_details, 'dp', split_axis=0, concat_axis=0, tiled=True)  9.2 us
  transfers between devices with their start and end apart: 15, of which 13 were waited for; matrix products, arithmetic and copies ran while one was open for 5% of the time, Pallas kernels for 0%

commit v1 on v0

--- a/solution.py
+++ b/solution.py
@@ -1,36 +1,163 @@
 import jax
 import jax.numpy as jnp
 from jax import lax
+from jax.experimental import pallas as pl
+from jax.experimental.pallas import tpu as pltpu
 from jax.sharding import PartitionSpec as P
 
 HEAD = 128
 DOC = 32
 SLOT = 8
-MICRO = 8
-
-
-def from_behind(shard, axis, by):
-    length = lax.axis_size(axis)
-    pairs = [(i, i + by) for i in range(length) if 0 <= i + by < length]
-    return lax.ppermute(shard, axis, pairs)
-
-
-def attend(block, gains):
-    rows, width = block.shape
-    heads = width // HEAD
-    values = block.reshape(rows // DOC, DOC, heads, HEAD)
-    widened = values.astype(jnp.float32)
-    square_mean = jnp.mean(widened * widened, axis=-1, keepdims=True)
-    normed = widened * lax.rsqrt(square_mean + 1e-06) * gains.reshape(heads, HEAD)
-    scores = jnp.einsum("dqhe,dkhe->dhqk", normed, normed, precision=lax.Precision.HIGHEST) * (
-        2.0 / HEAD
-    )
-    query_pos = lax.broadcasted_iota(jnp.int32, (DOC, DOC), 0)
-    key_pos = lax.broadcasted_iota(jnp.int32, (DOC, DOC), 1)
-    weights = jnp.where(key_pos <= query_pos, jnp.exp(scores), 0.0)
-    weights = (weights / jnp.sum(weights, axis=-1, keepdims=True)).astype(jnp.bfloat16)
-    mixed = jnp.einsum("dhqk,dkhe->dqhe", weights, values, preferred_element_type=jnp.float32)
-    return mixed.reshape(rows, width).astype(jnp.bfloat16)
+ROWS = 32
+SECTIONS = 4
+
+
+def attend(x, gains):
+    rows = x.shape[0]
+    row = lax.broadcasted_iota(jnp.int32, (rows, rows), 0)
+    col = lax.broadcasted_iota(jnp.int32, (rows, rows), 1)
+    allowed = (col <= row) & (col // DOC == row // DOC)
+    heads = []
+    for head in range(x.shape[1] // HEAD):
+        values = x[:, head * HEAD : (head + 1) * HEAD]
+        widened = values.astype(jnp.float32)
+        mean = jnp.mean(widened * widened, axis=-1, keepdims=True)
+        gain = gains[:, head * HEAD : (head + 1) * HEAD]
+        normed = (widened * lax.rsqrt(mean + 1e-06) * gain).astype(jnp.bfloat16)
+        scores = lax.dot_general(
+            normed, normed, (((1,), (1,)), ((), ())), preferred_element_type=jnp.float32
+        )
+        weights = jnp.where(allowed, jnp.exp(scores * (2.0 / HEAD)), 0.0)
+        weights = weights / jnp.sum(weights, axis=-1, keepdims=True)
+        heads.append(
+            jnp.dot(
+                weights.astype(jnp.bfloat16), values, preferred_element_type=jnp.float32
+            ).astype(jnp.bfloat16)
+        )
+    return jnp.concatenate(heads, axis=1)
+
+
+def blocks_kernel(
+    embedded, weight, gain, out, hidden, mixed, hidden_sem, mixed_sem, out_sent, mixed_sent
+):
+    section, tensor = lax.axis_index("section"), lax.axis_index("tensor")
+    micros = hidden.shape[0] // ROWS
+    peers = mixed.shape[0]
+    width = hidden.shape[1]
+    following = lax.rem(section + 1, SECTIONS)
+
+    def rows(micro):
+        return pl.ds(pl.multiple_of(micro * ROWS, ROWS), ROWS)
+
+    def relay(micro):
+        return pltpu.make_async_remote_copy(
+            src_ref=out.at[rows(micro)],
+            dst_ref=hidden.at[rows(micro)],
+            send_sem=out_sent.at[micro],
+            recv_sem=hidden_sem.at[micro],
+            device_id={"section": following},
+            device_id_type=pl.DeviceIdType.MESH,
+        )
+
+    def share(micro, step):
+        return pltpu.make_async_remote_copy(
+            src_ref=mixed.at[tensor, rows(micro)],
+            dst_ref=mixed.at[tensor, rows(micro)],
+            send_sem=mixed_sent.at[micro, step - 1],
+            recv_sem=mixed_sem.at[micro, step - 1],
+            device_id={"tensor": lax.rem(tensor + step, peers)},
+            device_id_type=pl.DeviceIdType.MESH,
+        )
+
+    barrier = pltpu.get_barrier_semaphore()
+    for step in range(1, peers):
+        pl.semaphore_signal(
+            barrier,
+            inc=1,
+            device_id={"tensor": lax.rem(tensor + step, peers)},
+            device_id_type=pl.DeviceIdType.MESH,
+        )
+    pl.semaphore_signal(
+        barrier,
+        inc=1,
+        device_id={"section": lax.rem(section + SECTIONS - 1, SECTIONS)},
+        device_id_type=pl.DeviceIdType.MESH,
+    )
+    pl.semaphore_wait(barrier, peers)
+
+    @pl.when(section == 0)
+    def _():
+        hidden[...] = embedded[...]
+
+    def mix(micro):
+        @pl.when(section > 0)
+        def _():
+            relay(micro).wait_recv()
+
+        mixed[tensor, rows(micro)] = attend(hidden[rows(micro)], gain[...])
+        for step in range(1, peers):
+            share(micro, step).start()
+
+    def project(micro):
+        for step in range(1, peers):
+            share(micro, step).wait_recv()
+        total = hidden[rows(micro)].astype(jnp.float32)
+        for peer in range(peers):
+            total += jnp.dot(
+                mixed[peer, rows(micro)],
+                weight[peer * width : (peer + 1) * width],
+                preferred_element_type=jnp.float32,
+            )
+        out[rows(micro)] = total.astype(jnp.bfloat16)
+
+        @pl.when(section < SECTIONS - 1)
+        def _():
+            relay(micro).start()
+
+    mix(0)
+
+    def step(micro, carry):
+        mix(micro)
+        project(micro - 1)
+        return carry
+
+    lax.fori_loop(1, micros, step, 0)
+    project(micros - 1)
+
+    def drain(micro, carry):
+        for step in range(1, peers):
+            share(micro, step).wait_send()
+
+        @pl.when(section < SECTIONS - 1)
+        def _():
+            relay(micro).wait_send()
+
+        return carry
+
+    lax.fori_loop(0, micros, drain, 0)
+
+
+def run_blocks(embedded, weight, gain, peers):
+    rows, width = embedded.shape
+    micros = rows // ROWS
+    vmem = pl.BlockSpec(memory_space=pltpu.VMEM)
+    return pl.pallas_call(
+        blocks_kernel,
+        out_shape=jax.ShapeDtypeStruct((rows, width), jnp.bfloat16),
+        in_specs=[vmem] * 3,
+        out_specs=vmem,
+        scratch_shapes=[
+            pltpu.VMEM((rows, width), jnp.bfloat16),
+            pltpu.VMEM((peers, rows, width), jnp.bfloat16),
+            pltpu.SemaphoreType.DMA((micros,)),
+            pltpu.SemaphoreType.DMA((micros, peers - 1)),
+            pltpu.SemaphoreType.DMA((micros,)),
+            pltpu.SemaphoreType.DMA((micros, peers - 1)),
+        ],
+        compiler_params=pltpu.CompilerParams(
+            collective_id=0, has_side_effects=True, vmem_limit_bytes=40 * 1024 * 1024
+        ),
+    )(embedded, weight, gain)
 
 
 def on_device(
@@ -104,32 +231,7 @@
         select_mat.T, returned.reshape(slots, SLOT * width), preferred_element_type=jnp.float32
     )
     image_grad = gathered_back.astype(jnp.bfloat16).reshape(samples * SLOT, width)
-    section_index = lax.axis_index("section")
-    section_count = lax.axis_size("section")
-    micro_rows = shard_rows // MICRO
-    incoming = jnp.zeros((micro_rows, width), jnp.bfloat16)
-    outputs = jnp.zeros((shard_rows, width), jnp.bfloat16)
-    step_count = MICRO + section_count - 1
-    for step in range(step_count):
-        lower = min(step, MICRO - 1) * micro_rows
-        first_rows = embedded[lower : lower + micro_rows]
-        block = jnp.where(section_index == 0, first_rows, incoming)
-        mixed = attend(block, gains)
-        total = block.astype(jnp.float32) + jnp.dot(
-            lax.all_gather(mixed, "tensor", axis=1, tiled=True),
-            out_full,
-            preferred_element_type=jnp.float32,
-        )
-        result = total.astype(jnp.bfloat16)
-        micro_index = step - section_index
-        active = (micro_index >= 0) & (micro_index < MICRO)
-        place_at = jnp.clip(micro_index, 0, MICRO - 1) * micro_rows
-        current = lax.dynamic_slice_in_dim(outputs, place_at, micro_rows, 0)
-        outputs = lax.dynamic_update_slice_in_dim(
-            outputs, jnp.where(active, result, current), place_at, 0
-        )
-        if step + 1 < step_count:
-            incoming = from_behind(result, "section", 1)
+    outputs = run_blocks(embedded, out_full, gains[None], lax.axis_size("tensor"))
     return (outputs[None], image_grad)
 
 

time: 443 us -> 274 us (0.62)
  blocking collectives: 136 us -> 27.7 us
  Pallas kernels: 0 us -> 72.1 us
  matrix products: 55.1 us -> 5.47 us
  waiting for transfers between devices: 182 us -> 136 us
  starting transfers between devices: 40.3 us -> 7.89 us
    all_gather x11 -> x0, blocking collectives: 136 us -> none  [on_device(): lax.all_gather(mixed, 'tensor', axis=1, tiled=True)]
    pallas_call x0 -> x1, Pallas kernels: none -> 72.1 us  [run_blocks(): pl.pallas_call(blocks_kernel, out_shape=jax.ShapeDtypeStruct((rows, width...]
    dot_general x33 -> x0, matrix products: 49.7 us -> none  [the longest x11 43.9 us: on_device(): jnp.dot(lax.all_gather(mixed, 'tensor', axis=1, tiled=True), out_full, pr...]
    ppermute x10 -> x0, waiting for transfers between devices: 42.5 us -> none  [from_behind(): return lax.ppermute(shard, axis, pairs)]
    all_to_all x1, waiting for transfers between devices: 0.01 us -> 32.9 us  [on_device(): lax.all_to_all(returned.reshape(dp_devices, pairs * SLOT, width), 'dp', s...]
    all_to_all x0 -> x1, blocking collectives: none -> 27.7 us  [on_device(): lax.all_to_all(slot_details, 'dp', split_axis=0, concat_axis=0, tiled=True)]
    all_to_all x1 -> x0, starting transfers between devices: 15.5 us -> none  [on_device(): lax.all_to_all(slot_details, 'dp', split_axis=0, concat_axis=0, tiled=True)]
    all_gather x1, waiting for transfers between devices: 59.5 us -> 45.5 us  [on_device(): lax.all_gather(out_weight[0], 'dp', axis=0, tiled=True)]
  transfers between devices with their start and end apart: 15 -> 4, of which waited for: 13 -> 3; matrix products, arithmetic and copies ran while one was open for 5% -> 4% of each run, Pallas kernels for 0% -> 0%
where the time goes in v1:
time: 274 us; the launch traced here: 273 us
  waiting for transfers between devices  136 us (50%)
  Pallas kernels  72.1 us (26%)
  blocking collectives  27.7 us (10%)
  between operations  14.1 us (5%)
  starting transfers between devices  7.89 us (3%)
  local copies, waits for them, and re-layouts  7.27 us (3%)
  matrix products  5.47 us (2%)
    pallas_call x1, Pallas kernels, run_blocks(): pl.pallas_call(blocks_kernel, out_shape=jax.ShapeDtypeStruct((rows, width...  72.1 us
    all_to_all x1, waiting for transfers between devices, on_device(): lax.all_to_all(outgoing, 'dp', split_axis=0, concat_axis=0, tiled=True)  56.3 us
    all_gather x1, waiting for transfers between devices, on_device(): lax.all_gather(out_weight[0], 'dp', axis=0, tiled=True)  45.5 us
    all_to_all x1, waiting for transfers between devices, on_device(): lax.all_to_all(returned.reshape(dp_devices, pairs * SLOT, width), 'dp', s...  32.9 us
    all_to_all x1, blocking collectives, on_device(): lax.all_to_all(slot_details, 'dp', split_axis=0, concat_axis=0, tiled=True)  27.7 us
  transfers between devices with their start and end apart: 4, of which 3 were waited for; matrix products, arithmetic and copies ran while one was open for 4% of the time, Pallas kernels for 0%

profile of v1, /device:TPU:6, one launch (start us, length us, event | category | flops | bytes accessed | tf_op | source)
XLA Modules:
  0.0 273.4 jit_solution(12313387210591703667)
XLA Ops:
  7.2 0.0 copy-start
  7.2 0.0 all-gather.4.cloned.1.call-start
  7.2 0.7 all-gather.4.cloned.1.call-update
  7.9 0.0 all-gather.6.cloned.1.call-start
  8.0 0.7 all-gather.6.cloned.1.call-update
  8.7 0.9 convert_reduce_fusion
  9.6 0.7 add.18
  10.2 0.7 pad_add_fusion
  10.9 0.1 iota_compare_fusion.4
  11.0 0.1 select_reduce_fusion
  11.1 0.1 copy.16
  11.2 27.7 %all_to_all.15 = s32[32,1,2]{2,1,0:T(1,128)S(1)} all-to-all(s32[32,1,2]{2,1,0:T(1,128)S(1)} %copy.16), channel_id=1, replica_groups=mesh['section'=4,'dp'=32,'tensor'=4] {'dp'}, dimensions={0} | all-to-all | bytes 512 | tf_op jit(solution)/shard_map/all_to_all | solution.py:202
  38.9 0.1 copy.17
  39.0 0.1 add_select_fusion
  39.1 0.1 select_n.21
  39.2 0.0 copy-done
  39.2 1.1 fusion
  40.3 3.9 %all-to-all-start.2 = ((bf16[32,8,896]{2,1,0:T(8,128)(2,1)}), bf16[32,8,896]{2,1,0:T(8,128)(2,1)S(1)}, u32[]{:S(2)}, u32[]{:S(2)}) async-start(bf16[32,8,896]{2,1,0:T(8,128)(2,1)} %fusion), calls=%async_computation.2 | async-start | bytes 917504 | tf_op jit(solution)/shard_map/all_to_all | solution.py:223
  44.2 1.1 reshape.80
  45.3 0.0 copy-start.3
  45.3 0.5 convolution_convert_fusion
  45.8 1.5 copy.18
  47.4 32.9 %all-to-all-done.2 = bf16[32,8,896]{2,1,0:T(8,128)(2,1)S(1)} async-done(((bf16[32,8,896]{2,1,0:T(8,128)(2,1)}), bf16[32,8,896]{2,1,0:T(8,128)(2,1)S(1)}, u32[]{:S(2)}, u32[]{:S(2)}) %all-to-all-start.2) | async-done | bytes 458784 | tf_op jit(solution)/shard_map/all_to_all | solution.py:223
  80.3 3.9 %all-to-all-start.1 = ((bf16[32,8,2048]{2,1,0:T(8,128)(2,1)}), bf16[32,8,2048]{2,1,0:T(8,128)(2,1)S(1)}, u32[]{:S(2)}, u32[]{:S(2)}) async-start(bf16[32,8,2048]{2,1,0:T(8,128)(2,1)} %bitcast.11), calls=%async_computation.1 | async-start | bytes 2097152 | tf_op jit(solution)/shard_map/all_to_all | solution.py:201
  84.3 0.1 fusion.4
  84.4 0.1 copy.19
  84.4 0.2 convolution_convert_fusion.1
  84.7 0.0 copy-start.2
  84.7 0.7 reshape.85
  85.4 56.3 %all-to-all-done.1 = bf16[32,8,2048]{2,1,0:T(8,128)(2,1)S(1)} async-done(((bf16[32,8,2048]{2,1,0:T(8,128)(2,1)}), bf16[32,8,2048]{2,1,0:T(8,128)(2,1)S(1)}, u32[]{:S(2)}, u32[]{:S(2)}) %all-to-all-start.1) | async-done | bytes 1048608 | tf_op jit(solution)/shard_map/all_to_all | solution.py:201
  141.7 0.0 all-gather.4.cloned.1.call-done
  141.7 0.0 copy-done.3
  141.7 3.6 %fusion.1.embedded = bf16[256,896]{1,0:T(8,128)(2,1)S(1)} fusion(bf16[256,896]{1,0:T(8,128)(2,1)S(1)} %copy-done.3, bf16[2048,896]{1,0:T(8,128)(2,1)} %all-gather.4.cloned.1.call-done, bf16[32,8,2048]{2,1,0:T(8,128)(2,1)S(1)} %all-to-all-done.1, pred[256]{0:T(512)(128)(4,1)S(1)} %fusion.4, s32[256]{0:T(256)S(1)} %select_n.21), kind=kOutput, calls=%fused_computation.6 | convolution fusion | flops 1057718272 | bytes 5637376 | tf_op jit(solution)/shard_map/dot_general | solution.py:216
  145.3 45.5 %all-gather.6.cloned.1.call-done = bf16[1,3584,896]{2,1,0:T(8,128)(2,1)} async-done(((bf16[1,112,896]{2,1,0:T(8,128)(2,1)}), bf16[1,3584,896]{2,1,0:T(8,128)(2,1)}) %all-gather.6.cloned.1.call-update) | async-done | bytes 6422544 | tf_op jit(solution)/shard_map/all_gather | solution.py:175
  190.8 0.0 copy-done.2
  190.8 0.0 copy-start.1
  190.8 2.8 %copy-done.1 = bf16[1,3584,896]{2,1,0:T(8,128)(2,1)S(1)} copy-done((bf16[1,3584,896]{2,1,0:T(8,128)(2,1)S(1)}, bf16[1,3584,896]{2,1,0:T(8,128)(2,1)}, u32[]{:S(2)}) %copy-start.1) | copy-done | bytes 6422552
  193.6 72.1 %shard_map.104 = bf16[256,896]{1,0:T(8,128)(2,1)S(1)} custom-call(bf16[256,896]{1,0:T(8,128)(2,1)S(1)} %fusion.1.embedded, bf16[3584,896]{1,0:T(8,128)(2,1)S(1)} %bitcast.24, f32[1,896]{1,0:T(1,128)S(1)} %copy-done.2), custom_call_target="tpu_custom_call" | custom-call | tf_op jit(solution)/shard_map/pallas_call | solution.py:144
  265.8 0.8 copy.21
  (1 shorter events, 0.0 us)
Async XLA Ops:
  7.2 32.0 %copy-start = (bf16[256,896]{1,0:T(8,128)(2,1)S(1)}, bf16[256,896]{1,0:T(8,128)(2,1)}, u32[]{:S(2)}) copy-start(bf16[256,896]{1,0:T(8,128)(2,1)} %param.17) | copy-start | bytes 1376260
  7.2 134.5 %all-gather.4.cloned.1.call-start = ((), (), s32[]{:S(2)}) async-start(), calls=%async_computation.3 | async-start | bytes 3784704 | tf_op jit(solution)/shard_map/all_gather | solution.py:176
  7.9 182.9 %all-gather.6.cloned.1.call-start = ((), (), s32[]{:S(2)}) async-start(), calls=%async_computation.4 | async-start | bytes 6623232 | tf_op jit(solution)/shard_map/all_gather | solution.py:175
  40.3 40.0 %all-to-all-start.2 = ((bf16[32,8,896]{2,1,0:T(8,128)(2,1)}), bf16[32,8,896]{2,1,0:T(8,128)(2,1)S(1)}, u32[]{:S(2)}, u32[]{:S(2)}) async-start(bf16[32,8,896]{2,1,0:T(8,128)(2,1)} %fusion), calls=%async_computation.2 | async-start | bytes 917504 | tf_op jit(solution)/shard_map/all_to_all | solution.py:223
  45.3 96.4 %copy-start.3 = (bf16[256,896]{1,0:T(8,128)(2,1)S(1)}, bf16[256,896]{1,0:T(8,128)(2,1)}, u32[]{:S(2)}) copy-start(bf16[256,896]{1,0:T(8,128)(2,1)} %param.9) | copy-start | bytes 1376260
  80.3 61.4 %all-to-all-start.1 = ((bf16[32,8,2048]{2,1,0:T(8,128)(2,1)}), bf16[32,8,2048]{2,1,0:T(8,128)(2,1)S(1)}, u32[]{:S(2)}, u32[]{:S(2)}) async-start(bf16[32,8,2048]{2,1,0:T(8,128)(2,1)} %bitcast.11), calls=%async_computation.1 | async-start | bytes 2097152 | tf_op jit(solution)/shard_map/all_to_all | solution.py:201
  84.7 106.1 %copy-start.2 = (f32[1,896]{1,0:T(1,128)S(1)}, f32[1,896]{1,0:T(1,128)}, u32[]{:S(2)}) copy-start(f32[1,896]{1,0:T(1,128)} %gain.1) | copy-start | bytes 10756
  190.8 2.8 %copy-start.1 = (bf16[1,3584,896]{2,1,0:T(8,128)(2,1)S(1)}, bf16[1,3584,896]{2,1,0:T(8,128)(2,1)}, u32[]{:S(2)}) copy-start(bf16[1,3584,896]{2,1,0:T(8,128)(2,1)} %all-gather.6.cloned.1.call-done) | copy-start | bytes 19267588
Sparse Core Ops, SparseCore 0:
  10.1 99.5 all-gather.3
  111.9 78.8 all-gather.5

commit v2 on v1

v2 whole, which is shorter than its diff:
```python
import jax
import jax.numpy as jnp
from jax import lax
from jax.experimental import pallas as pl
from jax.experimental.pallas import tpu as pltpu
from jax.sharding import PartitionSpec as P

HEAD = 128
DOC = 32
SLOT = 8
SAMP = 8
ROWS = 32
SECTIONS = 4
PEERS = 4
DP = 32
CHIPS = 16
PART = 256
HALF = 128
WEIGHT_CUTS = ((0, 64), (64, 48))
TILES = ((0, 0), (0, 1), (1, 0), (1, 1), (2, 0), (2, 1), (3, 1))
MESH = pl.DeviceIdType.MESH
BF16 = jnp.bfloat16
F32 = jnp.float32


def attend(x, gains):
    rows = x.shape[0]
    row = lax.broadcasted_iota(jnp.int32, (rows, rows), 0)
    col = lax.broadcasted_iota(jnp.int32, (rows, rows), 1)
    allowed = (col <= row) & (col // DOC == row // DOC)
    heads = []
    for head in range(x.shape[1] // HEAD):
        values = x[:, head * HEAD : (head + 1) * HEAD]
        widened = values.astype(jnp.float32)
        mean = jnp.mean(widened * widened, axis=-1, keepdims=True)
        gain = gains[:, head * HEAD : (head + 1) * HEAD]
        normed = (widened * lax.rsqrt(mean + 1e-06) * gain).astype(jnp.bfloat16)
        scores = lax.dot_general(
            normed, normed, (((1,), (1,)), ((), ())), preferred_element_type=jnp.float32
        )
        weights = jnp.where(allowed, jnp.exp(scores * (2.0 / HEAD)), 0.0)
        weights = weights / jnp.sum(weights, axis=-1, keepdims=True)
        heads.append(
            jnp.dot(
                weights.astype(jnp.bfloat16), values, preferred_element_type=jnp.float32
            ).astype(jnp.bfloat16)
        )
    return jnp.concatenate(heads, axis=1)


def iota(shape, dim):
    return lax.broadcasted_iota(jnp.int32, shape, dim)


def spread(index, scalars):
    total = jnp.zeros(index.shape, jnp.int32)
    for i in range(SAMP):
        total = jnp.where(index == i, scalars[i], total)
    return total


def wait_bytes(ref, sem):
    pltpu.make_async_copy(ref, ref, sem).wait()


def whole_kernel(
    text,
    vision,
    proj,
    shard_weight,
    gain,
    counts,
    dests,
    offsets,
    cotangent,
    out,
    image_grad,
    proj_ring,
    weight,
    outgoing,
    arrived,
    compact,
    returning,
    back,
    grads,
    hidden,
    mixed,
    proj_sem,
    proj_near,
    proj_sent,
    weight_sem,
    weight_near,
    weight_sent,
    route_sem,
    route_sent,
    back_sem,
    back_sent,
    compact_sem,
    compact_sent,
    grads_sem,
    grads_sent,
    hidden_sem,
    mixed_sem,
    out_sent,
    mixed_sent,
):
    section, tensor = lax.axis_index("section"), lax.axis_index("tensor")
    me = lax.axis_index("dp")
    chip, core = lax.div(me, 2), lax.rem(me, 2)
    width = hidden.shape[1]
    micros = hidden.shape[0] // ROWS
    following = lax.rem(section + 1, SECTIONS)
    right = lax.rem(chip + 1, CHIPS) * 2 + core
    left = lax.rem(chip + CHIPS - 1, CHIPS) * 2 + core
    near = chip * 2 + 1 - core
    first_column = pl.multiple_of(section * PART - lax.div(section, 3) * HALF, HALF)

    barrier = pltpu.get_barrier_semaphore()
    for device in (right, left, near):
        pl.semaphore_signal(barrier, inc=1, device_id={"dp": device}, device_id_type=MESH)
    for step in range(1, 4):
        pl.semaphore_signal(
            barrier, inc=1, device_id={"tensor": lax.rem(tensor + step, PEERS)}, device_id_type=MESH
        )
        pl.semaphore_signal(
            barrier,
            inc=1,
            device_id={"section": lax.rem(section + step, SECTIONS)},
            device_id_type=MESH,
        )

    dest = [dests[i] for i in range(SAMP)]
    offset = [offsets[i] for i in range(SAMP)]
    count = [counts[i] for i in range(SAMP)]
    table_row, table_lane = iota((2 * SAMP, PART), 0), iota((2 * SAMP, PART), 1)
    table = jnp.where(
        table_row < SAMP,
        spread(table_row, dest),
        jnp.where(
            table_lane < HALF, spread(table_row - SAMP, offset), spread(table_row - SAMP, count)
        ),
    )
    depth = proj.shape[0]
    proj_ring[me, pl.ds(0, depth)] = proj[:, pl.ds(first_column, PART)]
    proj_ring[me, pl.ds(depth, 2 * SAMP)] = table.astype(F32).astype(BF16)
    own = pl.multiple_of(me * shard_weight.shape[0], 16)
    weight[pl.ds(own, shard_weight.shape[0])] = shard_weight[...]
    pl.semaphore_wait(barrier, 9)

    def send(ref, sent, arrival, device):
        pltpu.make_async_remote_copy(
            src_ref=ref,
            dst_ref=ref,
            send_sem=sent,
            recv_sem=arrival,
            device_id={"dp": device},
            device_id_type=MESH,
        ).start()

    def landed(ref, sent, arrival):
        pltpu.make_async_remote_copy(
            src_ref=ref,
            dst_ref=ref,
            send_sem=sent,
            recv_sem=arrival,
            device_id={"dp": near},
            device_id_type=MESH,
        ).wait_recv()

    def proj_block(slot):
        return proj_ring.at[slot]

    def weight_block(slot, cut):
        start = pl.multiple_of(slot * shard_weight.shape[0] + cut[0], 16)
        return weight.at[pl.ds(start, cut[1])]

    def ring_start(block, arrival, sent, near_sem):
        for device in (right, left):
            send(block(me), sent, arrival(me), device)
        send(block(me), sent, near_sem, near)

    def ring_step(hop, block, arrival, sent, near_sem):
        from_left = lax.rem(chip + CHIPS - hop, CHIPS) * 2 + core
        from_right = lax.rem(chip + hop, CHIPS) * 2 + core
        if hop < CHIPS // 2:
            landed(block(from_left), sent, arrival(from_left))
            if hop < CHIPS // 2 - 1:
                send(block(from_left), sent, arrival(from_left), right)
            else:

                @pl.when(core == 0)
                def _():
                    send(block(from_left), sent, arrival(from_left), right)

            landed(block(from_right), sent, arrival(from_right))
            if hop < CHIPS // 2 - 1:
                send(block(from_right), sent, arrival(from_right), left)
            else:

                @pl.when(core == 1)
                def _():
                    send(block(from_right), sent, arrival(from_right), left)

            send(block(from_left), sent, near_sem, near)
            send(block(from_right), sent, near_sem, near)
        else:
            landed(block(from_left), sent, arrival(from_left))
            send(block(from_left), sent, near_sem, near)

    def weight_args(index):
        cut = WEIGHT_CUTS[index]
        return (
            lambda slot: weight_block(slot, cut),
            lambda slot: weight_sem.at[index, slot],
            weight_sent,
            weight_near,
        )

    def weight_step(hop):
        for index in range(len(WEIGHT_CUTS)):
            ring_step(hop, *weight_args(index))

    def proj_step(hop):
        ring_step(hop, *proj_args)

    proj_args = (proj_block, lambda slot: proj_sem.at[slot], proj_sent, proj_near)

    ring_start(*proj_args)
    for index in range(len(WEIGHT_CUTS)):
        ring_start(*weight_args(index))
    proj_step(1)
    proj_step(2)
    weight_step(1)
    proj_step(3)
    proj_step(4)
    proj_step(5)
    weight_step(2)
    proj_step(6)
    proj_step(7)
    proj_step(8)
    wait_bytes(proj_ring.at[pl.ds(0, CHIPS)], proj_near)

    full = proj_ring[:, 0:depth, :].reshape(DP * depth, PART)
    image = jnp.dot(vision[...], full, preferred_element_type=F32).astype(BF16)
    folded = jnp.concatenate([image[:, :HALF], image[:, HALF:]], axis=0)
    place, lane = iota((DP * 16, HALF), 0), iota((DP * 16, HALF), 1)
    lane_sample = lax.shift_right_logical(lane & 63, 3)
    picks = (lax.shift_right_logical(place, 4) == spread(lane_sample, dest)) & (
        (place & 15) == lax.shift_right_logical(lane, 6) * SLOT + (lane & 7)
    )
    slots = jnp.dot(picks.astype(F32).astype(BF16), folded, preferred_element_type=F32)
    outgoing[...] = slots.astype(BF16).reshape(DP, 16, HALF)
    arrived[me] = outgoing[me]

    def scatter(source, target, sent, arrival):
        def one(step, carry):
            device = lax.rem(me + step, DP)
            pltpu.make_async_remote_copy(
                src_ref=source.at[device],
                dst_ref=target.at[me],
                send_sem=sent,
                recv_sem=arrival,
                device_id={"dp": device},
                device_id_type=MESH,
            ).start()
            return carry

        lax.fori_loop(1, DP, one, 0)

    scatter(outgoing, arrived, route_sent, route_sem)
    weight_step(3)

    tables = proj_ring[:, depth : depth + 2 * SAMP, :].astype(F32)
    chosen = jnp.sum(
        jnp.where(tables[:, :SAMP] == me.astype(F32), tables[:, SAMP:], 0.0), axis=1, keepdims=True
    ).astype(jnp.int32)
    start_row, row_count = chosen[:, :, :HALF], chosen[:, :, HALF:]
    shape = (DP, 16, HALF)
    inner, column = iota(shape, 1), iota(shape, 2)
    within = column & 7
    gathers = (
        (lax.shift_right_logical(start_row, 5) == lax.shift_right_logical(column & 63, 3))
        & (inner == lax.shift_right_logical(column, 6) * SLOT + within)
        & (within < row_count)
    )
    gathers = gathers.astype(F32).astype(BF16).reshape(DP * 16, HALF)
    wait_bytes(arrived.at[pl.ds(0, DP - 1)], route_sem)
    packed = lax.dot_general(
        gathers,
        arrived[...].reshape(DP * 16, HALF),
        (((0,), (0,)), ((), ())),
        preferred_element_type=F32,
    )
    compact[section] = packed.astype(BF16)

    def hand_in(source):
        return pltpu.make_async_remote_copy(
            src_ref=compact.at[source],
            dst_ref=compact.at[source],
            send_sem=compact_sent,
            recv_sem=compact_sem.at[source],
            device_id={"section": 0},
            device_id_type=MESH,
        )

    @pl.when(section > 0)
    def _():
        hand_in(section).start()

    weight_step(4)

    @pl.when(section == 0)
    def _():
        for source in range(1, SECTIONS):
            hand_in(source).wait_recv()
        mark = iota((DP, HALF), 1)
        of_doc = lax.shift_right_logical(start_row[:, 0], 5) == lax.shift_right_logical(mark, 3)
        doc_row = jnp.sum(jnp.where(of_doc, start_row[:, 0], 0), axis=0, keepdims=True)
        doc_count = jnp.sum(jnp.where(of_doc, row_count[:, 0], 0), axis=0, keepdims=True)
        rows, mark = iota((text.shape[0], HALF), 0), iota((text.shape[0], HALF), 1)
        puts = (rows == doc_row + (mark & 7)) & ((mark & 7) < doc_count) & (mark < SAMP * SLOT)
        puts = puts.astype(F32)
        taken = jnp.sum(puts, axis=1, keepdims=True) > 0.0
        puts = puts[:, : SAMP * SLOT].astype(BF16)
        for tile, (source, half) in enumerate(TILES):
            columns = slice(tile * HALF, (tile + 1) * HALF)
            rows_here = compact[source, half * SAMP * SLOT : (half + 1) * SAMP * SLOT]
            placed = jnp.dot(puts, rows_here, preferred_element_type=F32)
            hidden[:, columns] = jnp.where(
                taken, placed, text[:, columns].astype(F32)
            ).astype(BF16)

    weight_step(5)

    def send_back():
        shape = (DP, 16, text.shape[0])
        inner, row = iota(shape, 1), iota(shape, 2)
        start = jnp.concatenate([start_row] * (text.shape[0] // HALF), axis=2)
        length = jnp.concatenate([row_count] * (text.shape[0] // HALF), axis=2)
        low = (start + inner == row) & (inner < length)
        high = (start + inner - SLOT == row) & (inner >= SLOT) & (inner - SLOT < length)
        low = low.astype(F32).astype(BF16).reshape(DP * 16, text.shape[0])
        high = high.astype(F32).astype(BF16).reshape(DP * 16, text.shape[0])
        part = cotangent[:, pl.ds(first_column, PART)]
        rows = jnp.dot(low, part[:, :HALF], preferred_element_type=F32)
        rows += jnp.dot(high, part[:, HALF:], preferred_element_type=F32)
        returning[...] = rows.astype(BF16).reshape(DP, 16, HALF)
        back[me] = returning[me]
        scatter(returning, back, back_sent, back_sem)

    def exchange(step):
        return pltpu.make_async_remote_copy(
            src_ref=grads.at[section],
            dst_ref=grads.at[section],
            send_sem=grads_sent.at[step - 1],
            recv_sem=grads_sem.at[step - 1],
            device_id={"section": lax.rem(section + step, SECTIONS)},
            device_id_type=MESH,
        )

    def collect():
        wait_bytes(back.at[pl.ds(0, DP - 1)], back_sem)
        shape = (2 * SAMP * SLOT, DP * 16)
        row, place = iota(shape, 0), iota(shape, 1)
        sample = lax.shift_right_logical(row & 63, 3)
        wants = (lax.shift_right_logical(place, 4) == spread(sample, dest)) & (
            (place & 15) == lax.shift_right_logical(row, 6) * SLOT + (row & 7)
        )
        grads[section] = jnp.dot(
            wants.astype(F32).astype(BF16),
            back[...].reshape(DP * 16, HALF),
            preferred_element_type=F32,
        ).astype(BF16)
        for step in range(1, SECTIONS):
            exchange(step).start()

    def rows_of(micro):
        return pl.ds(pl.multiple_of(micro * ROWS, ROWS), ROWS)

    def relay(micro):
        return pltpu.make_async_remote_copy(
            src_ref=out.at[rows_of(micro)],
            dst_ref=hidden.at[rows_of(micro)],
            send_sem=out_sent.at[micro],
            recv_sem=hidden_sem.at[micro],
            device_id={"section": following},
            device_id_type=MESH,
        )

    def share(micro, step):
        return pltpu.make_async_remote_copy(
            src_ref=mixed.at[tensor, rows_of(micro)],
            dst_ref=mixed.at[tensor, rows_of(micro)],
            send_sem=mixed_sent.at[micro, step - 1],
            recv_sem=mixed_sem.at[micro, step - 1],
            device_id={"tensor": lax.rem(tensor + step, PEERS)},
            device_id_type=MESH,
        )

    def mix(micro):
        mixed[tensor, rows_of(micro)] = attend(hidden[rows_of(micro)], gain[...])
        for step in range(1, PEERS):
            share(micro, step).start()

    def project(micro):
        for step in range(1, PEERS):
            share(micro, step).wait_recv()
        total = hidden[rows_of(micro)].astype(F32)
        for peer in range(PEERS):
            total += jnp.dot(
                mixed[peer, rows_of(micro)],
                weight[peer * width : (peer + 1) * width],
                preferred_element_type=F32,
            )
        out[rows_of(micro)] = total.astype(BF16)

        @pl.when(section < SECTIONS - 1)
        def _():
            relay(micro).start()

    def mix_some(first, last):
        @pl.when(section == 0)
        def _():
            def one(micro, carry):
                mix(micro)
                return carry

            lax.fori_loop(first, last, one, 0)

    mix_some(0, micros // 2)

    @pl.when(section > 0)
    def _():
        send_back()

    weight_step(6)
    mix_some(micros // 2, micros)
    weight_step(7)

    @pl.when(section > 0)
    def _():
        collect()

    weight_step(8)
    wait_bytes(weight.at[pl.ds(0, CHIPS * shard_weight.shape[0])], weight_near)

    def step(turn, carry):
        @pl.when((section > 0) & (turn < micros))
        def _():
            relay(turn).wait_recv()
            mix(turn)

        @pl.when(turn > 0)
        def _():
            project(turn - 1)

        return carry

    lax.fori_loop(0, micros + 1, step, 0)

    @pl.when(section == 0)
    def _():
        send_back()
        collect()

    for step in range(1, SECTIONS):
        exchange(step).wait_recv()
    for tile, (source, half) in enumerate(TILES):
        image_grad[:, tile * HALF : (tile + 1) * HALF] = grads[
            source, half * SAMP * SLOT : (half + 1) * SAMP * SLOT
        ]

    wait_bytes(proj_ring.at[pl.ds(0, DP - 1)], proj_sent)
    wait_bytes(weight.at[pl.ds(0, (DP - 1) * shard_weight.shape[0])], weight_sent)
    wait_bytes(arrived.at[pl.ds(0, DP - 1)], route_sent)
    wait_bytes(arrived.at[pl.ds(0, DP - 1)], back_sent)

    @pl.when(section > 0)
    def _():
        hand_in(section).wait_send()

    for step in range(1, SECTIONS):
        exchange(step).wait_send()

    def drain(micro, carry):
        for step in range(1, PEERS):
            share(micro, step).wait_send()

        @pl.when(section < SECTIONS - 1)
        def _():
            relay(micro).wait_send()

        return carry

    lax.fori_loop(0, micros, drain, 0)


def on_device(
    text_embed,
    vision,
    proj_weight,
    out_weight,
    qk_gain,
    image_counts,
    sample_shard,
    sample_offset,
    embed_grad,
):
    rows, width = text_embed.shape
    micros = rows // ROWS
    depth = proj_weight.shape[0]
    vmem = pl.BlockSpec(memory_space=pltpu.VMEM)
    smem = pl.BlockSpec(memory_space=pltpu.SMEM)
    dma = pltpu.SemaphoreType.DMA
    outputs, image_grad = pl.pallas_call(
        whole_kernel,
        out_shape=(
            jax.ShapeDtypeStruct((rows, width), BF16),
            jax.ShapeDtypeStruct((vision.shape[0], width), BF16),
        ),
        in_specs=[vmem] * 5 + [smem] * 3 + [vmem],
        out_specs=(vmem, vmem),
        scratch_shapes=[
            pltpu.VMEM((DP, depth + 2 * SAMP, PART), BF16),
            pltpu.VMEM((DP * out_weight.shape[1], width), BF16),
            pltpu.VMEM((DP, 16, HALF), BF16),
            pltpu.VMEM((DP, 16, HALF), BF16),
            pltpu.VMEM((SECTIONS, 2 * SAMP * SLOT, HALF), BF16),
            pltpu.VMEM((DP, 16, HALF), BF16),
            pltpu.VMEM((DP, 16, HALF), BF16),
            pltpu.VMEM((SECTIONS, 2 * SAMP * SLOT, HALF), BF16),
            pltpu.VMEM((rows, width), BF16),
            pltpu.VMEM((PEERS, rows, width), BF16),
            dma((DP,)),
            dma,
            dma,
            dma((len(WEIGHT_CUTS), DP)),
            dma,
            dma,
            dma,
            dma,
            dma,
            dma,
            dma((SECTIONS,)),
            dma,
            dma((SECTIONS - 1,)),
            dma((SECTIONS - 1,)),
            dma((micros,)),
            dma((micros, PEERS - 1)),
            dma((micros,)),
            dma((micros, PEERS - 1)),
        ],
        compiler_params=pltpu.CompilerParams(
            collective_id=0, has_side_effects=True, vmem_limit_bytes=40 * 1024 * 1024
        ),
    )(
        text_embed,
        vision,
        proj_weight,
        out_weight[0],
        qk_gain,
        image_counts,
        sample_shard,
        sample_offset,
        embed_grad,
    )
    return (outputs[None], image_grad)


def solution(mesh):
    placed = (
        P("dp", "tensor"),
        P("dp", None),
        P("dp", "tensor"),
        P("section", "dp", "tensor"),
        P("section", "tensor"),
        P("dp"),
        P("dp"),
        P("dp"),
        P("dp", "tensor"),
    )
    return jax.shard_map(
        on_device,
        mesh=mesh,
        in_specs=placed,
        out_specs=(P("section", "dp", "tensor"), P("dp", "tensor")),
        check_vma=False,
    )
```

time: 274 us -> 150 us (0.55)
  waiting for transfers between devices: 136 us -> 0 us
  Pallas kernels: 72.1 us -> 142 us
  blocking collectives: 27.7 us -> 0 us
  between operations: 14.1 us -> 0.67 us
  starting transfers between devices: 7.89 us -> 0 us
  matrix products: 5.47 us -> 0 us
    all_to_all x2 -> x0, waiting for transfers between devices: 89.2 us -> none  [the longest x1 56.3 us: on_device(): lax.all_to_all(outgoing, 'dp', split_axis=0, concat_axis=0, tiled=True)]
    pallas_call x1, Pallas kernels: 72.1 us -> 142 us  [on_device(): pl.pallas_call(whole_kernel, out_shape=(jax.ShapeDtypeStruct((rows, width...]
    all_gather x2 -> x0, waiting for transfers between devices: 45.6 us -> none  [the longest x1 45.5 us: on_device(): lax.all_gather(out_weight[0], 'dp', axis=0, tiled=True)]
    all_to_all x1 -> x0, blocking collectives: 27.7 us -> none  [on_device(): lax.all_to_all(slot_details, 'dp', split_axis=0, concat_axis=0, tiled=True)]
    all_to_all x2 -> x0, starting transfers between devices: 7.81 us -> none  [the longest x1 3.93 us: on_device(): lax.all_to_all(outgoing, 'dp', split_axis=0, concat_axis=0, tiled=True)]
    dot_general x4 -> x0, matrix products: 5.47 us -> none  [the longest x1 3.58 us: on_device(): jnp.dot(placing_mat, image_slots, preferred_element_type=jnp.float32)]
    unnamed x11 -> x20, local copies, waits for them, and re-layouts: 5.21 us -> 7.57 us
  transfers between devices with their start and end apart: 4 -> 0, of which waited for: 3 -> 0; matrix products, arithmetic and copies ran while one was open for 4% -> 0% of each run, Pallas kernels for 0% -> 0%
where the time goes in v2:
time: 150 us
  Pallas kernels  142 us (95%)
  local copies, waits for them, and re-layouts  7.57 us (5%)
    pallas_call x1, Pallas kernels, on_device(): pl.pallas_call(whole_kernel, out_shape=(jax.ShapeDtypeStruct((rows, width...  142 us
    unnamed x20, local copies, waits for them, and re-layouts  7.57 us

profile of v2, /device:TPU:6, one launch (start us, length us, event | category | flops | bytes accessed | tf_op | source)
XLA Modules:
  0.0 149.9 jit_solution(11069668167593124692)
XLA Ops:
  0.6 0.0 copy-start.8
  0.6 0.0 copy-start.7
  0.7 0.0 copy-start.6
  0.7 0.6 copy-done.8
  1.3 0.0 copy-done.7
  1.3 0.0 copy-done.6
  1.3 0.0 copy-start
  1.3 1.0 copy-done
  2.3 0.0 copy-start.1
  2.3 1.0 copy-done.1
  3.4 0.0 copy-start.2
  3.4 0.9 copy-done.2
  4.3 0.0 copy-start.3
  4.3 0.9 copy-done.3
  5.2 0.0 copy-start.4
  5.2 0.9 copy-done.4
  6.1 0.0 copy-start.5
  6.1 0.7 copy-done.5
  6.8 141.7 %shard_map.104 = (bf16[256,896]{1,0:T(8,128)(2,1)S(1)}, bf16[64,896]{1,0:T(8,128)(2,1)S(1)}) custom-call(bf16[256,896]{1,0:T(8,128)(2,1)S(1)} %copy-done, bf16[64,2048]{1,0:T(8,128)(2,1)S(1)} %copy-done.2, bf16[64,896]{1,0:T(8,128)(2,1)S(1)} %copy-done.4, bf16[112,896]{1,0:T(8,128)(2,1)S(1)} %bitcast.3, f32[1,896]{1,0:T(1,128)S(1)} %copy-done.5, ...), custom_call_target="tpu_custom_call" | custom-call | tf_op jit(solution)/shard_map/pallas_call | solution.py:515
  148.5 0.8 copy.13
  149.3 0.6 copy.14
Async XLA Ops:
  0.6 0.7 copy-start.8
  0.6 0.7 copy-start.7
  0.7 0.7 copy-start.6
  1.3 1.0 copy-start
  2.3 1.0 copy-start.1
  3.4 0.9 copy-start.2
  4.3 0.9 copy-start.3
  5.2 0.9 copy-start.4
  6.1 0.7 copy-start.5

commit v3 on v2

v3 whole, which is shorter than its diff:
```python
import jax
import jax.numpy as jnp
from jax import lax
from jax.experimental import pallas as pl
from jax.experimental.pallas import tpu as pltpu
from jax.sharding import PartitionSpec as P

HEAD = 128
DOC = 32
SLOT = 8
SAMP = 8
ROWS = 32
SECTIONS = 4
PEERS = 4
DP = 32
CHIPS = 16
PIECES = 16
HALF = 128
FRONT = 512
FOLDED = 64
PLACERS = 2
WEIGHT_CUTS = ((0, 64), (64, 48))
IMAGE_TILES = ((2, 0), (2, 1), (2, 2), (2, 3), (3, 1), (3, 2), (3, 3))
TILES = ((1, 0), (1, 1), (2, 0), (2, 1), (3, 0), (3, 1), (3, 2))
MESH = pl.DeviceIdType.MESH
BF16 = jnp.bfloat16
F32 = jnp.float32


def attend(x, gains):
    rows = x.shape[0]
    row, col = iota((rows, rows), 0), iota((rows, rows), 1)
    allowed = (col <= row) & (lax.div(col, DOC) == lax.div(row, DOC))
    cuts = [slice(first, first + HEAD) for first in range(0, x.shape[1], HEAD)]
    values = [x[:, cut] for cut in cuts]
    wide = [value.astype(F32) for value in values]
    means = [jnp.mean(value * value, axis=-1, keepdims=True) for value in wide]
    normed = [
        (value * lax.rsqrt(mean + 1e-06) * gains[:, cut]).astype(BF16)
        for value, mean, cut in zip(wide, means, cuts)
    ]
    scores = [
        lax.dot_general(each, each, (((1,), (1,)), ((), ())), preferred_element_type=F32)
        for each in normed
    ]
    weights = [jnp.where(allowed, jnp.exp(score * (2.0 / HEAD)), 0.0) for score in scores]
    weights = [(each / jnp.sum(each, axis=-1, keepdims=True)).astype(BF16) for each in weights]
    mixed = [
        jnp.dot(each, value, preferred_element_type=F32).astype(BF16)
        for each, value in zip(weights, values)
    ]
    return jnp.concatenate(mixed, axis=1)


def iota(shape, dim):
    return lax.broadcasted_iota(jnp.int32, shape, dim)


def spread(index, scalars):
    total = jnp.zeros(index.shape, jnp.int32)
    for i in range(SAMP):
        total = jnp.where(index == i, scalars[i], total)
    return total


def wait_bytes(ref, sem):
    pltpu.make_async_copy(ref, ref, sem).wait()


def whole_kernel(
    text,
    vision,
    proj,
    shard_weight,
    gain_input,
    counts,
    dests,
    offsets,
    cotangent_input,
    out,
    image_grad,
    gain,
    vision_part,
    cotangent,
    proj_ring,
    weight,
    outgoing,
    arrived,
    pieces,
    images,
    returning,
    back,
    hidden,
    mixed,
    load_sem,
    pieces_sem,
    pieces_sent,
    rows_sem,
    rows_sent,
    proj_sem,
    proj_near,
    proj_sent,
    weight_sem,
    weight_near,
    weight_sent,
    route_sem,
    route_sent,
    back_sem,
    back_sent,
    images_sem,
    images_sent,
    grads_sem,
    grads_sent,
    hidden_sem,
    mixed_sem,
    out_sent,
    mixed_sent,
):
    section, tensor = lax.axis_index("section"), lax.axis_index("tensor")
    me = lax.axis_index("dp")
    chip, core = lax.div(me, 2), lax.rem(me, 2)
    width = hidden.shape[1]
    micros = hidden.shape[0] // ROWS
    following = lax.rem(section + 1, SECTIONS)
    right = lax.rem(chip + 1, CHIPS) * 2 + core
    left = lax.rem(chip + CHIPS - 1, CHIPS) * 2 + core
    near = chip * 2 + 1 - core
    image_column = pl.multiple_of(lax.div(section, 3) * 3 * HALF, HALF)
    piece = section * PEERS + tensor
    depth, share_rows = proj.shape[0], shard_weight.shape[0]

    def load(source, target, index):
        return pltpu.make_async_copy(source, target, load_sem.at[index])

    own = pl.multiple_of(me * share_rows, 16)
    load_weight = load(shard_weight, weight.at[pl.ds(own, share_rows)], 0)
    load_vision = load(
        vision.at[:, pl.ds(pl.multiple_of(piece * HALF, HALF), HALF)], vision_part, 1
    )
    load_cotangent = load(cotangent_input, cotangent, 2)
    load_text = load(text, hidden, 3)
    load_proj = load(proj.at[:, pl.ds(image_column, FRONT)], proj_ring.at[me], 4)
    load_gain = load(gain_input, gain, 5)
    load_weight.start()
    load_gain.start()
    load_vision.start()

    @pl.when(section >= PLACERS)
    def _():
        load_proj.start()

    barrier = pltpu.get_barrier_semaphore()

    def greet(step, carry):
        pl.semaphore_signal(
            barrier, inc=1, device_id={"dp": lax.rem(me + step, DP)}, device_id_type=MESH
        )
        return carry

    lax.fori_loop(1, DP, greet, 0)
    for step in range(1, 4):
        pl.semaphore_signal(
            barrier, inc=1, device_id={"tensor": lax.rem(tensor + step, PEERS)}, device_id_type=MESH
        )
        pl.semaphore_signal(
            barrier,
            inc=1,
            device_id={"section": lax.rem(section + step, SECTIONS)},
            device_id_type=MESH,
        )

    @pl.when(section == 0)
    def _():
        load_text.start()
        load_cotangent.start()

    dest = [dests[i] for i in range(SAMP)]
    offset = [offsets[i] for i in range(SAMP)]
    count = [counts[i] for i in range(SAMP)]

    row = iota((HALF - SAMP * SLOT, HALF), 0)
    table = jnp.where(row < SAMP, spread(row, offset), spread(row - SAMP, count))
    table = table.astype(F32).astype(BF16)
    place, lane = iota((DP * 16, HALF), 0), iota((DP * 16, HALF), 1)
    is_row = lane < SAMP * SLOT
    lane_sample = jnp.where(is_row, lax.shift_right_logical(lane, 3), lane & 7)
    lane_inner = jnp.where(is_row, lane & 7, lax.shift_right_logical(lane, 3))
    picks = (
        (lax.shift_right_logical(place, 4) == spread(lane_sample, dest))
        & ((place & 15) == lane_inner)
        & (lane < SAMP * SLOT + 2 * SAMP)
    )
    load_vision.wait()
    slots = jnp.dot(
        picks.astype(F32).astype(BF16),
        jnp.concatenate([vision_part[...], table], axis=0),
        preferred_element_type=F32,
    )
    outgoing[...] = slots.astype(BF16).reshape(DP, 16, HALF)
    arrived[me] = outgoing[me]
    load_weight.wait()
    load_gain.wait()

    @pl.when(section >= PLACERS)
    def _():
        load_proj.wait()

    pl.semaphore_wait(barrier, DP - 1 + 6)

    def send(ref, sent, arrival, device):
        pltpu.make_async_remote_copy(
            src_ref=ref,
            dst_ref=ref,
            send_sem=sent,
            recv_sem=arrival,
            device_id={"dp": device},
            device_id_type=MESH,
        ).start()

    def landed(ref, sent, arrival):
        pltpu.make_async_remote_copy(
            src_ref=ref,
            dst_ref=ref,
            send_sem=sent,
            recv_sem=arrival,
            device_id={"dp": near},
            device_id_type=MESH,
        ).wait_recv()

    def proj_block(slot):
        return proj_ring.at[slot]

    def weight_block(slot, cut):
        start = pl.multiple_of(slot * share_rows + cut[0], 16)
        return weight.at[pl.ds(start, cut[1])]

    def ring_start(block, arrival, sent, near_sem):
        for device in (right, left):
            send(block(me), sent, arrival(me), device)
        send(block(me), sent, near_sem, near)

    def ring_step(hop, block, arrival, sent, near_sem):
        from_left = lax.rem(chip + CHIPS - hop, CHIPS) * 2 + core
        from_right = lax.rem(chip + hop, CHIPS) * 2 + core
        if hop < CHIPS // 2:
            landed(block(from_left), sent, arrival(from_left))
            if hop < CHIPS // 2 - 1:
                send(block(from_left), sent, arrival(from_left), right)
            else:

                @pl.when(core == 0)
                def _():
                    send(block(from_left), sent, arrival(from_left), right)

            landed(block(from_right), sent, arrival(from_right))
            if hop < CHIPS // 2 - 1:
                send(block(from_right), sent, arrival(from_right), left)
            else:

                @pl.when(core == 1)
                def _():
                    send(block(from_right), sent, arrival(from_right), left)

            send(block(from_left), sent, near_sem, near)
            send(block(from_right), sent, near_sem, near)
        else:
            landed(block(from_left), sent, arrival(from_left))
            send(block(from_left), sent, near_sem, near)

    def weight_args(index):
        cut = WEIGHT_CUTS[index]
        return (
            lambda slot: weight_block(slot, cut),
            lambda slot: weight_sem.at[index, slot],
            weight_sent,
            weight_near,
        )

    def weight_step(hop):
        for index in range(len(WEIGHT_CUTS)):
            ring_step(hop, *weight_args(index))

    def proj_step(hop):
        ring_step(hop, *proj_args)

    proj_args = (proj_block, lambda slot: proj_sem.at[slot], proj_sent, proj_near)

    def scatter(source, target, sent, arrival):
        def one(step, carry):
            device = lax.rem(me + step, DP)
            pltpu.make_async_remote_copy(
                src_ref=source.at[device],
                dst_ref=target.at[me],
                send_sem=sent,
                recv_sem=arrival,
                device_id={"dp": device},
                device_id_type=MESH,
            ).start()
            return carry

        lax.fori_loop(1, DP, one, 0)

    def weight_start():
        for index in range(len(WEIGHT_CUTS)):
            ring_start(*weight_args(index))

    @pl.when(section >= PLACERS)
    def _():
        ring_start(*proj_args)

    @pl.when(section < PLACERS)
    def _():
        weight_start()

    scatter(outgoing, arrived, route_sent, route_sem)

    def of_sources():
        message = arrived[:, SLOT : SLOT + 2, :].astype(F32).astype(jnp.int32)
        return message[:, 0:1], message[:, 1:2]

    def gather_piece(step):
        return pltpu.make_async_remote_copy(
            src_ref=pieces.at[piece],
            dst_ref=pieces.at[piece],
            send_sem=pieces_sent.at[step - 1],
            recv_sem=pieces_sem.at[step - 1],
            device_id={"tensor": lax.rem(tensor + step, PEERS)},
            device_id_type=MESH,
        )

    def pack():
        wait_bytes(arrived.at[pl.ds(0, DP - 1)], route_sem)
        start_row, row_count = of_sources()
        shape = (DP, 16, HALF)
        inner, column = iota(shape, 1), iota(shape, 2)
        gathers = (
            (lax.shift_right_logical(start_row, 5) == lax.shift_right_logical(column, 3))
            & (inner == (column & 7))
            & (inner < row_count)
        )
        packed = lax.dot_general(
            gathers.astype(F32).astype(BF16).reshape(DP * 16, HALF),
            arrived[...].reshape(DP * 16, HALF),
            (((0,), (0,)), ((), ())),
            preferred_element_type=F32,
        )
        pieces[piece] = packed[: SAMP * SLOT].astype(BF16)
        for step in range(1, PEERS):
            gather_piece(step).start()

    def gather_rows(step):
        mine = pieces.at[pl.ds(section * PEERS, PEERS)]
        return pltpu.make_async_remote_copy(
            src_ref=mine,
            dst_ref=mine,
            send_sem=rows_sent.at[step - 1],
            recv_sem=rows_sem.at[step - 1],
            device_id={"section": lax.rem(section + step, SECTIONS)},
            device_id_type=MESH,
        )

    def pass_pieces():
        for step in range(1, PEERS):
            gather_piece(step).wait_recv()
        for step in range(1, SECTIONS):

            @pl.when(lax.rem(section + step, SECTIONS) >= PLACERS)
            def _():
                gather_rows(step).start()

    def hand_in(source):
        return pltpu.make_async_remote_copy(
            src_ref=images.at[source],
            dst_ref=images.at[source],
            send_sem=images_sent,
            recv_sem=images_sem.at[source],
            device_id={"section": 0},
            device_id_type=MESH,
        )

    def make_images():
        wait_bytes(proj_ring.at[pl.ds(0, CHIPS)], proj_near)
        for step in range(1, SECTIONS):
            gather_rows(step).wait_recv()
        image = jnp.dot(
            jnp.concatenate([pieces[index] for index in range(PIECES)], axis=1),
            proj_ring[...].reshape(DP * depth, FRONT),
            preferred_element_type=F32,
        )
        images[section] = image.astype(BF16)
        hand_in(section).start()

    def place_images():
        start_row, row_count = of_sources()
        start_row, row_count = start_row[:, 0], row_count[:, 0]
        mark = iota((DP, HALF), 1)
        of_doc = lax.shift_right_logical(start_row, 5) == lax.shift_right_logical(mark, 3)
        doc_row = jnp.sum(jnp.where(of_doc, start_row, 0), axis=0, keepdims=True)
        doc_count = jnp.sum(jnp.where(of_doc, row_count, 0), axis=0, keepdims=True)
        rows, mark = iota((text.shape[0], HALF), 0), iota((text.shape[0], HALF), 1)
        puts = (rows == doc_row + (mark & 7)) & ((mark & 7) < doc_count) & (mark < SAMP * SLOT)
        puts = puts.astype(F32)
        taken = jnp.sum(puts, axis=1, keepdims=True) > 0.0
        puts = puts[:, : SAMP * SLOT].astype(BF16)
        load_text.wait()
        for source in range(PLACERS, SECTIONS):
            hand_in(source).wait_recv()
        for tile, (source, part) in enumerate(IMAGE_TILES):
            columns = slice(tile * HALF, (tile + 1) * HALF)
            placed = jnp.dot(
                puts,
                images[source, :, part * HALF : (part + 1) * HALF],
                preferred_element_type=F32,
            )
            hidden[:, columns] = jnp.where(
                taken, placed, hidden[:, columns].astype(F32)
            ).astype(BF16)

    def send_back():
        load_cotangent.wait()
        start_row, row_count = of_sources()
        total = text.shape[0]
        start_row = jnp.concatenate([start_row] * (total // HALF), axis=2)
        row_count = jnp.concatenate([row_count] * (total // HALF), axis=2)
        shape = (DP, SLOT, total)
        inner, row = iota(shape, 1), iota(shape, 2)
        takes = (start_row + inner == row) & (inner < row_count)
        rows = jnp.dot(
            takes.astype(F32).reshape(DP * SLOT, total).astype(BF16),
            cotangent[...],
            preferred_element_type=F32,
        ).reshape(DP, SLOT, width)
        tiles = [rows[:, :, first : first + HALF] for first in range(0, width, HALF)]
        spare = jnp.zeros((DP, FOLDED - SLOT * len(tiles), HALF), F32)
        returning[...] = jnp.concatenate(tiles + [spare], axis=1).astype(BF16)
        back[me] = returning[me]
        scatter(returning, back, back_sent, back_sem)

    def exchange(step):
        return pltpu.make_async_remote_copy(
            src_ref=image_grad,
            dst_ref=image_grad,
            send_sem=grads_sent.at[step - 1],
            recv_sem=grads_sem,
            device_id={"section": step},
            device_id_type=MESH,
        )

    def collect():
        wait_bytes(back.at[pl.ds(0, DP - 1)], back_sem)
        found = [back[dest[i]].astype(F32) for i in range(SAMP)]
        for tile in range(width // HALF):
            rows = [each[tile * SLOT : (tile + 1) * SLOT] for each in found]
            image_grad[:, tile * HALF : (tile + 1) * HALF] = jnp.concatenate(
                rows, axis=0
            ).astype(BF16)
        for step in range(1, SECTIONS):
            exchange(step).start()

    def rows_of(micro):
        return pl.ds(pl.multiple_of(micro * ROWS, ROWS), ROWS)

    def relay(micro):
        return pltpu.make_async_remote_copy(
            src_ref=out.at[rows_of(micro)],
            dst_ref=hidden.at[rows_of(micro)],
            send_sem=out_sent.at[micro],
            recv_sem=hidden_sem.at[micro],
            device_id={"section": following},
            device_id_type=MESH,
        )

    def share(micro, step):
        return pltpu.make_async_remote_copy(
            src_ref=mixed.at[tensor, rows_of(micro)],
            dst_ref=mixed.at[tensor, rows_of(micro)],
            send_sem=mixed_sent.at[micro, step - 1],
            recv_sem=mixed_sem.at[micro, step - 1],
            device_id={"tensor": lax.rem(tensor + step, PEERS)},
            device_id_type=MESH,
        )

    def mix(micro):
        mixed[tensor, rows_of(micro)] = attend(hidden[rows_of(micro)], gain[...])
        for step in (2, 1, 3):
            share(micro, step).start()

    def project(micro):
        total = hidden[rows_of(micro)].astype(F32)
        for step in (0, 1, 3, 2):
            if step > 0:
                share(micro, step).wait_recv()
            peer = lax.rem(tensor + PEERS - step, PEERS)
            total += jnp.dot(
                mixed[peer, rows_of(micro)],
                weight[pl.ds(pl.multiple_of(peer * width, HEAD), width)],
                preferred_element_type=F32,
            )
        out[rows_of(micro)] = total.astype(BF16)

        @pl.when(section < SECTIONS - 1)
        def _():
            relay(micro).start()

    def mix_some(first, last):
        def one(micro, carry):
            mix(micro)
            return carry

        lax.fori_loop(first, last, one, 0)

    @pl.when(section < PLACERS)
    def _():
        weight_step(1)
        weight_step(2)
        pack()
        weight_step(3)
        pass_pieces()
        for hop in range(4, 8):
            weight_step(hop)

    @pl.when(section == 0)
    def _():
        place_images()
        mix_some(0, micros // 2)

    @pl.when(section < PLACERS)
    def _():
        weight_step(8)

    @pl.when(section == 0)
    def _():
        mix_some(micros // 2, micros)

    @pl.when(section >= PLACERS)
    def _():
        def weight_early(hop, first):
            @pl.when(section == first)
            def _():
                if hop == 0:
                    weight_start()
                else:
                    weight_step(hop)

        proj_step(1)
        proj_step(2)
        proj_step(3)
        weight_early(0, 2)
        pack()
        proj_step(4)
        pass_pieces()
        proj_step(5)
        proj_step(6)
        weight_early(1, 2)
        proj_step(7)
        weight_early(0, 3)
        proj_step(8)
        weight_early(2, 2)
        make_images()
        weight_early(1, 3)
        weight_early(2, 3)
        for hop in range(3, 9):
            weight_step(hop)

    wait_bytes(weight.at[pl.ds(0, CHIPS * share_rows)], weight_near)

    def step(turn, carry):
        @pl.when((section > 0) & (turn < micros))
        def _():
            relay(turn).wait_recv()
            mix(turn)

        @pl.when(turn > 0)
        def _():
            project(turn - 1)

        return carry

    lax.fori_loop(0, micros + 1, step, 0)

    @pl.when(section == 0)
    def _():
        send_back()
        collect()
        wait_bytes(returning.at[pl.ds(0, DP - 1)], back_sent)
        for step in range(1, SECTIONS):
            exchange(step).wait_send()

    @pl.when(section > 0)
    def _():
        exchange(1).wait_recv()

    wait_bytes(weight.at[pl.ds(0, (DP - 1) * share_rows)], weight_sent)
    wait_bytes(arrived.at[pl.ds(0, DP - 1)], route_sent)

    @pl.when(section >= PLACERS)
    def _():
        wait_bytes(proj_ring.at[pl.ds(0, DP - 1)], proj_sent)
        hand_in(section).wait_send()

    for step in range(1, PEERS):
        gather_piece(step).wait_send()
    for step in range(1, SECTIONS):

        @pl.when(lax.rem(section + step, SECTIONS) >= PLACERS)
        def _():
            gather_rows(step).wait_send()

    def drain(micro, carry):
        for step in range(1, PEERS):
            share(micro, step).wait_send()

        @pl.when(section < SECTIONS - 1)
        def _():
            relay(micro).wait_send()

        return carry

    lax.fori_loop(0, micros, drain, 0)


def on_device(
    text_embed,
    vision,
    proj_weight,
    out_weight,
    qk_gain,
    image_counts,
    sample_shard,
    sample_offset,
    embed_grad,
):
    rows, width = text_embed.shape
    micros = rows // ROWS
    depth = proj_weight.shape[0]
    vmem = pl.BlockSpec(memory_space=pltpu.VMEM)
    hbm = pl.BlockSpec(memory_space=pl.ANY)
    smem = pl.BlockSpec(memory_space=pltpu.SMEM)
    dma = pltpu.SemaphoreType.DMA
    outputs, image_grad = pl.pallas_call(
        whole_kernel,
        out_shape=(
            jax.ShapeDtypeStruct((rows, width), BF16),
            jax.ShapeDtypeStruct((vision.shape[0], width), BF16),
        ),
        in_specs=[hbm] * 5 + [smem] * 3 + [hbm],
        out_specs=(vmem, vmem),
        scratch_shapes=[
            pltpu.VMEM((1, width), F32),
            pltpu.VMEM((vision.shape[0], HALF), BF16),
            pltpu.VMEM((rows, width), BF16),
            pltpu.VMEM((DP, depth, FRONT), BF16),
            pltpu.VMEM((DP * out_weight.shape[1], width), BF16),
            pltpu.VMEM((DP, 16, HALF), BF16),
            pltpu.VMEM((DP, 16, HALF), BF16),
            pltpu.VMEM((PIECES, SAMP * SLOT, HALF), BF16),
            pltpu.VMEM((SECTIONS, SAMP * SLOT, FRONT), BF16),
            pltpu.VMEM((DP, FOLDED, HALF), BF16),
            pltpu.VMEM((DP, FOLDED, HALF), BF16),
            pltpu.VMEM((rows, width), BF16),
            pltpu.VMEM((PEERS, rows, width), BF16),
            dma((6,)),
            dma((PEERS - 1,)),
            dma((PEERS - 1,)),
            dma((SECTIONS - 1,)),
            dma((SECTIONS - 1,)),
            dma((DP,)),
            dma,
            dma,
            dma((len(WEIGHT_CUTS), DP)),
            dma,
            dma,
            dma,
            dma,
            dma,
            dma,
            dma((SECTIONS,)),
            dma,
            dma,
            dma((SECTIONS - 1,)),
            dma((micros,)),
            dma((micros, PEERS - 1)),
            dma((micros,)),
            dma((micros, PEERS - 1)),
        ],
        compiler_params=pltpu.CompilerParams(
            collective_id=0, has_side_effects=True, vmem_limit_bytes=60 * 1024 * 1024
        ),
    )(
        text_embed,
        vision,
        proj_weight,
        out_weight[0],
        qk_gain,
        image_counts,
        sample_shard,
        sample_offset,
        embed_grad,
    )
    return (outputs[None], image_grad)


def solution(mesh):
    placed = (
        P("dp", "tensor"),
        P("dp", None),
        P("dp", "tensor"),
        P("section", "dp", "tensor"),
        P("section", "tensor"),
        P("dp"),
        P("dp"),
        P("dp"),
        P("dp", "tensor"),
    )
    return jax.shard_map(
        on_device,
        mesh=mesh,
        in_specs=placed,
        out_specs=(P("section", "dp", "tensor"), P("dp", "tensor")),
        check_vma=False,
    )
```

time: 150 us -> 120 us (0.80)
  Pallas kernels: 142 us -> 116 us
  local copies, waits for them, and re-layouts: 7.57 us -> 2.51 us
    pallas_call x1, Pallas kernels: 142 us -> 116 us  [on_device(): pl.pallas_call(whole_kernel, out_shape=(jax.ShapeDtypeStruct((rows, width...]
    unnamed x20 -> x4, local copies, waits for them, and re-layouts: 7.57 us -> 2.51 us
where the time goes in v3:
time: 120 us
  Pallas kernels  116 us (97%)
  local copies, waits for them, and re-layouts  2.51 us (2%)
    pallas_call x1, Pallas kernels, on_device(): pl.pallas_call(whole_kernel, out_shape=(jax.ShapeDtypeStruct((rows, width...  116 us
    unnamed x4, local copies, waits for them, and re-layouts  2.51 us

profile of v3, /device:TPU:6, one launch (start us, length us, event | category | flops | bytes accessed | tf_op | source)
XLA Modules:
  0.0 119.6 jit_solution(6154575090155123496)
XLA Ops:
  0.6 116.5 %shard_map.104 = (bf16[256,896]{1,0:T(8,128)(2,1)}, bf16[64,896]{1,0:T(8,128)(2,1)}) custom-call(bf16[256,896]{1,0:T(8,128)(2,1)} %text.1, bf16[64,2048]{1,0:T(8,128)(2,1)} %vision.1, bf16[64,896]{1,0:T(8,128)(2,1)} %proj.1, bf16[112,896]{1,0:T(8,128)(2,1)} %bitcast.3, f32[1,896]{1,0:T(1,128)} %gain_input.1, s32[8]{0:T(128)} %counts.1, s32[8]{0:T(128)} %dests.1, ...), custom_call_target="tpu_custom_call" | custom-call | tf_op jit(solution)/shard_map/pallas_call | solution.py:640
  117.1 0.0 copy-start
  117.1 1.9 %copy.13 = bf16[1,256,896]{2,1,0:T(8,128)(2,1)} copy(bf16[1,256,896]{2,1,0:T(8,128)(2,1)} %bitcast.2) | data formatting | bytes 917504
  119.0 0.0 copy-done
  119.0 0.6 copy.14
Async XLA Ops:
  117.1 1.9 %copy-start = (bf16[64,896]{1,0:T(8,128)(2,1)S(1)}, bf16[64,896]{1,0:T(8,128)(2,1)}, u32[]{:S(2)}) copy-start(bf16[64,896]{1,0:T(8,128)(2,1)} %get-tuple-element.9) | copy-start | bytes 344068

commit v4 on v3

--- a/solution.py
+++ b/solution.py
@@ -18,6 +18,7 @@
 HALF = 128
 FRONT = 512
 FOLDED = 64
+BACK_TURN = 4
 PLACERS = 2
 WEIGHT_CUTS = ((0, 64), (64, 48))
 IMAGE_TILES = ((2, 0), (2, 1), (2, 2), (2, 3), (3, 1), (3, 2), (3, 3))
@@ -98,7 +99,6 @@
     rows_sem,
     rows_sent,
     proj_sem,
-    proj_near,
     proj_sent,
     weight_sem,
     weight_near,
@@ -178,6 +178,122 @@
     offset = [offsets[i] for i in range(SAMP)]
     count = [counts[i] for i in range(SAMP)]
 
+    load_weight.wait()
+
+    @pl.when(section >= PLACERS)
+    def _():
+        load_proj.wait()
+
+    pl.semaphore_wait(barrier, DP - 1 + 6)
+
+    def send(ref, sent, arrival, device):
+        pltpu.make_async_remote_copy(
+            src_ref=ref,
+            dst_ref=ref,
+            send_sem=sent,
+            recv_sem=arrival,
+            device_id={"dp": device},
+            device_id_type=MESH,
+        ).start()
+
+    def landed(ref, sent, arrival):
+        pltpu.make_async_remote_copy(
+            src_ref=ref,
+            dst_ref=ref,
+            send_sem=sent,
+            recv_sem=arrival,
+            device_id={"dp": near},
+            device_id_type=MESH,
+        ).wait_recv()
+
+    def proj_block(slot):
+        return proj_ring.at[slot]
+
+    def weight_block(slot, cut):
+        start = pl.multiple_of(slot * share_rows + cut[0], 16)
+        return weight.at[pl.ds(start, cut[1])]
+
+    def ring_start(block, arrival, sent, near_at):
+        for device in (right, left):
+            send(block(me), sent, arrival(me), device)
+        send(block(me), sent, near_at(me), near)
+
+    def ring_step(hop, block, arrival, sent, near_at):
+        from_left = lax.rem(chip + CHIPS - hop, CHIPS) * 2 + core
+        from_right = lax.rem(chip + hop, CHIPS) * 2 + core
+        if hop < CHIPS // 2:
+            landed(block(from_left), sent, arrival(from_left))
+            if hop < CHIPS // 2 - 1:
+                send(block(from_left), sent, arrival(from_left), right)
+            else:
+
+                @pl.when(core == 0)
+                def _():
+                    send(block(from_left), sent, arrival(from_left), right)
+
+            landed(block(from_right), sent, arrival(from_right))
+            if hop < CHIPS // 2 - 1:
+                send(block(from_right), sent, arrival(from_right), left)
+            else:
+
+                @pl.when(core == 1)
+                def _():
+                    send(block(from_right), sent, arrival(from_right), left)
+
+            send(block(from_left), sent, near_at(from_left), near)
+            send(block(from_right), sent, near_at(from_right), near)
+        else:
+            landed(block(from_left), sent, arrival(from_left))
+            send(block(from_left), sent, near_at(from_left), near)
+
+    def weight_args(index):
+        cut = WEIGHT_CUTS[index]
+        return (
+            lambda slot: weight_block(slot, cut),
+            lambda slot: weight_sem.at[index, slot],
+            weight_sent,
+            lambda slot: weight_near,
+        )
+
+    def weight_step(hop):
+        for index in range(len(WEIGHT_CUTS)):
+            ring_step(hop, *weight_args(index))
+
+    def proj_step(hop):
+        ring_step(hop, *proj_args)
+
+    def proj_arrival(slot):
+        return proj_sem.at[slot]
+
+    proj_args = (proj_block, proj_arrival, proj_sent, proj_arrival)
+
+    def scatter(source, target, sent, arrival):
+        def one(step, carry):
+            device = lax.rem(me + step, DP)
+            pltpu.make_async_remote_copy(
+                src_ref=source.at[device],
+                dst_ref=target.at[me],
+                send_sem=sent,
+                recv_sem=arrival,
+                device_id={"dp": device},
+                device_id_type=MESH,
+            ).start()
+            return carry
+
+        lax.fori_loop(1, DP, one, 0)
+
+    def weight_start():
+        for index in range(len(WEIGHT_CUTS)):
+            ring_start(*weight_args(index))
+
+    @pl.when(section >= PLACERS)
+    def _():
+        ring_start(*proj_args)
+
+    @pl.when(section < PLACERS)
+    def _():
+        weight_start()
+
     row = iota((HALF - SAMP * SLOT, HALF), 0)
     table = jnp.where(row < SAMP, spread(row, offset), spread(row - SAMP, count))
     table = table.astype(F32).astype(BF16)
@@ -198,121 +314,8 @@
     )
     outgoing[...] = slots.astype(BF16).reshape(DP, 16, HALF)
     arrived[me] = outgoing[me]
-    load_weight.wait()
+    scatter(outgoing, arrived, route_sent, route_sem)
     load_gain.wait()
-
-    @pl.when(section >= PLACERS)
-    def _():
-        load_proj.wait()
-
-    pl.semaphore_wait(barrier, DP - 1 + 6)
-
-    def send(ref, sent, arrival, device):
-        pltpu.make_async_remote_copy(
-            src_ref=ref,
-            dst_ref=ref,
-            send_sem=sent,
-            recv_sem=arrival,
-            device_id={"dp": device},
-            device_id_type=MESH,
-        ).start()
-
-    def landed(ref, sent, arrival):
-        pltpu.make_async_remote_copy(
-            src_ref=ref,
-            dst_ref=ref,
-            send_sem=sent,
-            recv_sem=arrival,
-            device_id={"dp": near},
-            device_id_type=MESH,
-        ).wait_recv()
-
-    def proj_block(slot):
-        return proj_ring.at[slot]
-
-    def weight_block(slot, cut):
-        start = pl.multiple_of(slot * share_rows + cut[0], 16)
-        return weight.at[pl.ds(start, cut[1])]
-
-    def ring_start(block, arrival, sent, near_sem):
-        for device in (right, left):
-            send(block(me), sent, arrival(me), device)
-        send(block(me), sent, near_sem, near)
-
-    def ring_step(hop, block, arrival, sent, near_sem):
-        from_left = lax.rem(chip + CHIPS - hop, CHIPS) * 2 + core
-        from_right = lax.rem(chip + hop, CHIPS) * 2 + core
-        if hop < CHIPS // 2:
-            landed(block(from_left), sent, arrival(from_left))
-            if hop < CHIPS // 2 - 1:
-                send(block(from_left), sent, arrival(from_left), right)
-            else:
-
-                @pl.when(core == 0)
-                def _():
-                    send(block(from_left), sent, arrival(from_left), right)
-
-            landed(block(from_right), sent, arrival(from_right))
-            if hop < CHIPS // 2 - 1:
-                send(block(from_right), sent, arrival(from_right), left)
-            else:
-
-                @pl.when(core == 1)
-                def _():
-                    send(block(from_right), sent, arrival(from_right), left)
-
-            send(block(from_left), sent, near_sem, near)
-            send(block(from_right), sent, near_sem, near)
-        else:
-            landed(block(from_left), sent, arrival(from_left))
-            send(block(from_left), sent, near_sem, near)
-
-    def weight_args(index):
-        cut = WEIGHT_CUTS[index]
-        return (
-            lambda slot: weight_block(slot, cut),
-            lambda slot: weight_sem.at[index, slot],
-            weight_sent,
-            weight_near,
-        )
-
-    def weight_step(hop):
-        for index in range(len(WEIGHT_CUTS)):
-            ring_step(hop, *weight_args(index))
-
-    def proj_step(hop):
-        ring_step(hop, *proj_args)
-
-    proj_args = (proj_block, lambda slot: proj_sem.at[slot], proj_sent, proj_near)
-
-    def scatter(source, target, sent, arrival):
-        def one(step, carry):
-            device = lax.rem(me + step, DP)
-            pltpu.make_async_remote_copy(
-                src_ref=source.at[device],
-                dst_ref=target.at[me],
-                send_sem=sent,
-                recv_sem=arrival,
-                device_id={"dp": device},
-                device_id_type=MESH,
-            ).start()
-            return carry
-
-        lax.fori_loop(1, DP, one, 0)
-
-    def weight_start():
-        for index in range(len(WEIGHT_CUTS)):
-            ring_start(*weight_args(index))
-
-    @pl.when(section >= PLACERS)
-    def _():
-        ring_start(*proj_args)
-
-    @pl.when(section < PLACERS)
-    def _():
-        weight_start()
-
-    scatter(outgoing, arrived, route_sent, route_sem)
 
     def of_sources():
         message = arrived[:, SLOT : SLOT + 2, :].astype(F32).astype(jnp.int32)
@@ -378,45 +381,48 @@
             device_id_type=MESH,
         )
 
-    def make_images():
-        wait_bytes(proj_ring.at[pl.ds(0, CHIPS)], proj_near)
-        for step in range(1, SECTIONS):
-            gather_rows(step).wait_recv()
-        image = jnp.dot(
-            jnp.concatenate([pieces[index] for index in range(PIECES)], axis=1),
-            proj_ring[...].reshape(DP * depth, FRONT),
-            preferred_element_type=F32,
-        )
-        images[section] = image.astype(BF16)
-        hand_in(section).start()
-
-    def place_images():
+    def times_columns(offsets):
+        total = None
+        for step in offsets:
+            there = lax.rem(chip + CHIPS + step, CHIPS)
+            other = there * 2 + 1 - core
+            landed(proj_block(other), proj_sent, proj_arrival(other))
+            term = jnp.dot(
+                pieces[there],
+                proj_ring[pl.ds(there * 2, 2)].reshape(2 * depth, FRONT),
+                preferred_element_type=F32,
+            )
+            total = term if total is None else total + term
+        return total
+
+    def doc_tables():
         start_row, row_count = of_sources()
         start_row, row_count = start_row[:, 0], row_count[:, 0]
         mark = iota((DP, HALF), 1)
         of_doc = lax.shift_right_logical(start_row, 5) == lax.shift_right_logical(mark, 3)
         doc_row = jnp.sum(jnp.where(of_doc, start_row, 0), axis=0, keepdims=True)
         doc_count = jnp.sum(jnp.where(of_doc, row_count, 0), axis=0, keepdims=True)
-        rows, mark = iota((text.shape[0], HALF), 0), iota((text.shape[0], HALF), 1)
-        puts = (rows == doc_row + (mark & 7)) & ((mark & 7) < doc_count) & (mark < SAMP * SLOT)
+        return doc_row, doc_count
+
+    def place(micro, doc_row, doc_count):
+        row, mark = iota((ROWS, HALF), 0) + micro * ROWS, iota((ROWS, HALF), 1)
+        puts = (row == doc_row + (mark & 7)) & ((mark & 7) < doc_count) & (mark < SAMP * SLOT)
         puts = puts.astype(F32)
         taken = jnp.sum(puts, axis=1, keepdims=True) > 0.0
         puts = puts[:, : SAMP * SLOT].astype(BF16)
-        load_text.wait()
-        for source in range(PLACERS, SECTIONS):
-            hand_in(source).wait_recv()
-        for tile, (source, part) in enumerate(IMAGE_TILES):
-            columns = slice(tile * HALF, (tile + 1) * HALF)
-            placed = jnp.dot(
+        here = pl.ds(pl.multiple_of(micro * ROWS, ROWS), ROWS)
+        placed = [
+            jnp.dot(
                 puts,
                 images[source, :, part * HALF : (part + 1) * HALF],
                 preferred_element_type=F32,
             )
-            hidden[:, columns] = jnp.where(
-                taken, placed, hidden[:, columns].astype(F32)
-            ).astype(BF16)
-
-    def send_back():
+            for source, part in IMAGE_TILES
+        ]
+        placed = jnp.concatenate(placed, axis=1)
+        hidden[here] = jnp.where(taken, placed, hidden[here].astype(F32)).astype(BF16)
+
+    def prepare_back():
         load_cotangent.wait()
         start_row, row_count = of_sources()
         total = text.shape[0]
@@ -434,7 +440,6 @@
         spare = jnp.zeros((DP, FOLDED - SLOT * len(tiles), HALF), F32)
         returning[...] = jnp.concatenate(tiles + [spare], axis=1).astype(BF16)
         back[me] = returning[me]
-        scatter(returning, back, back_sent, back_sem)
 
     def exchange(step):
         return pltpu.make_async_remote_copy(
@@ -503,7 +508,10 @@
             relay(micro).start()
 
     def mix_some(first, last):
+        doc_row, doc_count = doc_tables()
+
         def one(micro, carry):
+            place(micro, doc_row, doc_count)
             mix(micro)
             return carry
 
@@ -516,12 +524,20 @@
         pack()
         weight_step(3)
         pass_pieces()
-        for hop in range(4, 8):
+        weight_step(4)
+
+        @pl.when(section == 0)
+        def _():
+            prepare_back()
+
+        for hop in range(5, 8):
             weight_step(hop)
 
     @pl.when(section == 0)
     def _():
-        place_images()
+        load_text.wait()
+        for source in range(PLACERS, SECTIONS):
+            hand_in(source).wait_recv()
         mix_some(0, micros // 2)
 
     @pl.when(section < PLACERS)
@@ -542,24 +558,40 @@
                 else:
                     weight_step(hop)
 
+        def weight_early(hop, first):
+            @pl.when(section == first)
+            def _():
+                if hop == 0:
+                    weight_start()
+                else:
+                    weight_step(hop)
+
         proj_step(1)
+        weight_early(0, 2)
+        weight_early(0, 3)
         proj_step(2)
         proj_step(3)
-        weight_early(0, 2)
         pack()
         proj_step(4)
+        weight_early(1, 2)
+        weight_early(1, 3)
         pass_pieces()
         proj_step(5)
         proj_step(6)
-        weight_early(1, 2)
+        weight_early(2, 2)
+        weight_early(2, 3)
+        for step in range(1, SECTIONS):
+            gather_rows(step).wait_recv()
+        total = times_columns((0, 1, -1, 2, -2, 3, -3, 4, -4, 5, -5))
         proj_step(7)
-        weight_early(0, 3)
+        total += times_columns((6, -6))
         proj_step(8)
-        weight_early(2, 2)
-        make_images()
-        weight_early(1, 3)
-        weight_early(2, 3)
-        for hop in range(3, 9):
+        weight_early(3, 2)
+        weight_early(3, 3)
+        total += times_columns((7, -7, 8))
+        images[section] = total.astype(BF16)
+        hand_in(section).start()
+        for hop in range(4, 9):
             weight_step(hop)
 
     wait_bytes(weight.at[pl.ds(0, CHIPS * share_rows)], weight_near)
@@ -570,17 +602,20 @@
             relay(turn).wait_recv()
             mix(turn)
 
-        @pl.when(turn > 0)
+        @pl.when(turn > 1)
         def _():
-            project(turn - 1)
+            project(turn - 2)
+
+        @pl.when((section == 0) & (turn == BACK_TURN))
+        def _():
+            scatter(returning, back, back_sent, back_sem)
 
         return carry
 
-    lax.fori_loop(0, micros + 1, step, 0)
+    lax.fori_loop(0, micros + 2, step, 0)
 
     @pl.when(section == 0)
     def _():
-        send_back()
         collect()
         wait_bytes(returning.at[pl.ds(0, DP - 1)], back_sent)
         for step in range(1, SECTIONS):
@@ -666,7 +701,6 @@
             dma((SECTIONS - 1,)),
             dma((DP,)),
             dma,
-            dma,
             dma((len(WEIGHT_CUTS), DP)),
             dma,
             dma,

time: 120 us -> 117 us (0.975)
  Pallas kernels: 116 us -> 114 us
    pallas_call x1, Pallas kernels: 116 us -> 114 us  [on_device(): pl.pallas_call(whole_kernel, out_shape=(jax.ShapeDtypeStruct((rows, width...]
where the time goes in v4:
time: 117 us
  Pallas kernels  114 us (97%)
  local copies, waits for them, and re-layouts  2.51 us (2%)
    pallas_call x1, Pallas kernels, on_device(): pl.pallas_call(whole_kernel, out_shape=(jax.ShapeDtypeStruct((rows, width...  114 us
    unnamed x4, local copies, waits for them, and re-layouts  2.51 us

profile of v4, /device:TPU:6, one launch (start us, length us, event | category | flops | bytes accessed | tf_op | source)
XLA Modules:
  0.0 116.8 jit_solution(9881384773482095748)
XLA Ops:
  0.6 113.6 %shard_map.104 = (bf16[256,896]{1,0:T(8,128)(2,1)}, bf16[64,896]{1,0:T(8,128)(2,1)}) custom-call(bf16[256,896]{1,0:T(8,128)(2,1)} %text.1, bf16[64,2048]{1,0:T(8,128)(2,1)} %vision.1, bf16[64,896]{1,0:T(8,128)(2,1)} %proj.1, bf16[112,896]{1,0:T(8,128)(2,1)} %bitcast.3, f32[1,896]{1,0:T(1,128)} %gain_input.1, s32[8]{0:T(128)} %counts.1, s32[8]{0:T(128)} %dests.1, ...), custom_call_target="tpu_custom_call" | custom-call | tf_op jit(solution)/shard_map/pallas_call | solution.py:675
  114.3 0.0 copy-start
  114.3 1.9 %copy.13 = bf16[1,256,896]{2,1,0:T(8,128)(2,1)} copy(bf16[1,256,896]{2,1,0:T(8,128)(2,1)} %bitcast.2) | data formatting | bytes 917504
  116.1 0.0 copy-done
  116.1 0.6 copy.14
Async XLA Ops:
  114.3 1.9 %copy-start = (bf16[64,896]{1,0:T(8,128)(2,1)S(1)}, bf16[64,896]{1,0:T(8,128)(2,1)}, u32[]{:S(2)}) copy-start(bf16[64,896]{1,0:T(8,128)(2,1)} %get-tuple-element.9) | copy-start | bytes 344068

commit v5 on v4

--- a/solution.py
+++ b/solution.py
@@ -78,6 +78,8 @@
     dests,
     offsets,
     cotangent_input,
+    out_result,
+    image_grad_result,
     out,
     image_grad,
     gain,
@@ -94,6 +96,8 @@
     hidden,
     mixed,
     load_sem,
+    store_sem,
+    store_grad_sem,
     pieces_sem,
     pieces_sent,
     rows_sem,
@@ -371,12 +375,13 @@
             def _():
                 gather_rows(step).start()
 
-    def hand_in(source):
+    def hand_in(source, half):
+        part = images.at[source, pl.ds(half * SAMP * SLOT // 2, SAMP * SLOT // 2)]
         return pltpu.make_async_remote_copy(
-            src_ref=images.at[source],
-            dst_ref=images.at[source],
-            send_sem=images_sent,
-            recv_sem=images_sem.at[source],
+            src_ref=part,
+            dst_ref=part,
+            send_sem=images_sent.at[half],
+            recv_sem=images_sem.at[source, half],
             device_id={"section": 0},
             device_id_type=MESH,
         )
@@ -404,17 +409,18 @@
         doc_count = jnp.sum(jnp.where(of_doc, row_count, 0), axis=0, keepdims=True)
         return doc_row, doc_count
 
-    def place(micro, doc_row, doc_count):
+    def place(micro, half, doc_row, doc_count):
+        known = slice(half * SAMP * SLOT // 2, (half + 1) * SAMP * SLOT // 2)
         row, mark = iota((ROWS, HALF), 0) + micro * ROWS, iota((ROWS, HALF), 1)
         puts = (row == doc_row + (mark & 7)) & ((mark & 7) < doc_count) & (mark < SAMP * SLOT)
         puts = puts.astype(F32)
         taken = jnp.sum(puts, axis=1, keepdims=True) > 0.0
-        puts = puts[:, : SAMP * SLOT].astype(BF16)
+        puts = puts[:, known].astype(BF16)
         here = pl.ds(pl.multiple_of(micro * ROWS, ROWS), ROWS)
         placed = [
             jnp.dot(
                 puts,
-                images[source, :, part * HALF : (part + 1) * HALF],
+                images[source, known, part * HALF : (part + 1) * HALF],
                 preferred_element_type=F32,
             )
             for source, part in IMAGE_TILES
@@ -465,6 +471,11 @@
     def rows_of(micro):
         return pl.ds(pl.multiple_of(micro * ROWS, ROWS), ROWS)
 
+    def store(micro):
+        return pltpu.make_async_copy(
+            out.at[rows_of(micro)], out_result.at[rows_of(micro)], store_sem.at[micro]
+        )
+
     def relay(micro):
         return pltpu.make_async_remote_copy(
             src_ref=out.at[rows_of(micro)],
@@ -487,7 +498,7 @@
 
     def mix(micro):
         mixed[tensor, rows_of(micro)] = attend(hidden[rows_of(micro)], gain[...])
-        for step in (2, 1, 3):
+        for step in (1, 3, 2):
             share(micro, step).start()
 
     def project(micro):
@@ -502,20 +513,23 @@
                 preferred_element_type=F32,
             )
         out[rows_of(micro)] = total.astype(BF16)
+        store(micro).start()
 
         @pl.when(section < SECTIONS - 1)
         def _():
             relay(micro).start()
 
-    def mix_some(first, last):
+    def mix_some(half):
+        for source in range(PLACERS, SECTIONS):
+            hand_in(source, half).wait_recv()
         doc_row, doc_count = doc_tables()
 
         def one(micro, carry):
-            place(micro, doc_row, doc_count)
+            place(micro, half, doc_row, doc_count)
             mix(micro)
             return carry
 
-        lax.fori_loop(first, last, one, 0)
+        lax.fori_loop(half * micros // 2, (half + 1) * micros // 2, one, 0)
 
     @pl.when(section < PLACERS)
     def _():
@@ -536,9 +550,7 @@
     @pl.when(section == 0)
     def _():
         load_text.wait()
-        for source in range(PLACERS, SECTIONS):
-            hand_in(source).wait_recv()
-        mix_some(0, micros // 2)
+        mix_some(0)
 
     @pl.when(section < PLACERS)
     def _():
@@ -546,7 +558,7 @@
 
     @pl.when(section == 0)
     def _():
-        mix_some(micros // 2, micros)
+        mix_some(1)
 
     @pl.when(section >= PLACERS)
     def _():
@@ -558,28 +570,19 @@
                 else:
                     weight_step(hop)
 
-        def weight_early(hop, first):
-            @pl.when(section == first)
-            def _():
-                if hop == 0:
-                    weight_start()
-                else:
-                    weight_step(hop)
-
         proj_step(1)
         weight_early(0, 2)
-        weight_early(0, 3)
         proj_step(2)
         proj_step(3)
+        weight_early(0, 3)
         pack()
         proj_step(4)
         weight_early(1, 2)
-        weight_early(1, 3)
         pass_pieces()
         proj_step(5)
         proj_step(6)
         weight_early(2, 2)
-        weight_early(2, 3)
+        weight_early(1, 3)
         for step in range(1, SECTIONS):
             gather_rows(step).wait_recv()
         total = times_columns((0, 1, -1, 2, -2, 3, -3, 4, -4, 5, -5))
@@ -587,10 +590,12 @@
         total += times_columns((6, -6))
         proj_step(8)
         weight_early(3, 2)
-        weight_early(3, 3)
+        weight_early(2, 3)
         total += times_columns((7, -7, 8))
         images[section] = total.astype(BF16)
-        hand_in(section).start()
+        for half in range(2):
+            hand_in(section, half).start()
+        weight_early(3, 3)
         for hop in range(4, 9):
             weight_step(hop)
 
@@ -625,13 +630,17 @@
     def _():
         exchange(1).wait_recv()
 
+    store_grad = pltpu.make_async_copy(image_grad, image_grad_result, store_grad_sem)
+    store_grad.start()
+
     wait_bytes(weight.at[pl.ds(0, (DP - 1) * share_rows)], weight_sent)
     wait_bytes(arrived.at[pl.ds(0, DP - 1)], route_sent)
 
     @pl.when(section >= PLACERS)
     def _():
         wait_bytes(proj_ring.at[pl.ds(0, DP - 1)], proj_sent)
-        hand_in(section).wait_send()
+        for half in range(2):
+            hand_in(section, half).wait_send()
 
     for step in range(1, PEERS):
         gather_piece(step).wait_send()
@@ -642,6 +651,7 @@
             gather_rows(step).wait_send()
 
     def drain(micro, carry):
+        store(micro).wait()
         for step in range(1, PEERS):
             share(micro, step).wait_send()
 
@@ -652,6 +662,7 @@
         return carry
 
     lax.fori_loop(0, micros, drain, 0)
+    store_grad.wait()
 
 
 def on_device(
@@ -668,7 +679,6 @@
     rows, width = text_embed.shape
     micros = rows // ROWS
     depth = proj_weight.shape[0]
-    vmem = pl.BlockSpec(memory_space=pltpu.VMEM)
     hbm = pl.BlockSpec(memory_space=pl.ANY)
     smem = pl.BlockSpec(memory_space=pltpu.SMEM)
     dma = pltpu.SemaphoreType.DMA
@@ -679,8 +689,10 @@
             jax.ShapeDtypeStruct((vision.shape[0], width), BF16),
         ),
         in_specs=[hbm] * 5 + [smem] * 3 + [hbm],
-        out_specs=(vmem, vmem),
+        out_specs=(hbm, hbm),
         scratch_shapes=[
+            pltpu.VMEM((rows, width), BF16),
+            pltpu.VMEM((vision.shape[0], width), BF16),
             pltpu.VMEM((1, width), F32),
             pltpu.VMEM((vision.shape[0], HALF), BF16),
             pltpu.VMEM((rows, width), BF16),
@@ -695,6 +707,8 @@
             pltpu.VMEM((rows, width), BF16),
             pltpu.VMEM((PEERS, rows, width), BF16),
             dma((6,)),
+            dma((micros,)),
+            dma,
             dma((PEERS - 1,)),
             dma((PEERS - 1,)),
             dma((SECTIONS - 1,)),
@@ -708,8 +722,8 @@
             dma,
             dma,
             dma,
-            dma((SECTIONS,)),
-            dma,
+            dma((SECTIONS, 2)),
+            dma((2,)),
             dma,
             dma((SECTIONS - 1,)),
             dma((micros,)),

time: 117 us -> 114 us (0.974)
  Pallas kernels: 114 us -> 111 us
    pallas_call x1, Pallas kernels: 114 us -> 111 us  [on_device(): pl.pallas_call(whole_kernel, out_shape=(jax.ShapeDtypeStruct((rows, width...]
where the time goes in v5:
time: 114 us
  Pallas kernels  111 us (97%)
  local copies, waits for them, and re-layouts  2.51 us (2%)
    pallas_call x1, Pallas kernels, on_device(): pl.pallas_call(whole_kernel, out_shape=(jax.ShapeDtypeStruct((rows, width...  111 us
    unnamed x4, local copies, waits for them, and re-layouts  2.51 us

profile of v5, /device:TPU:6, one launch (start us, length us, event | category | flops | bytes accessed | tf_op | source)
XLA Modules:
  0.0 114.0 jit_solution(10778793252223089623)
XLA Ops:
  0.6 110.9 %shard_map.104 = (bf16[256,896]{1,0:T(8,128)(2,1)}, bf16[64,896]{1,0:T(8,128)(2,1)}) custom-call(bf16[256,896]{1,0:T(8,128)(2,1)} %text.1, bf16[64,2048]{1,0:T(8,128)(2,1)} %vision.1, bf16[64,896]{1,0:T(8,128)(2,1)} %proj.1, bf16[112,896]{1,0:T(8,128)(2,1)} %bitcast.3, f32[1,896]{1,0:T(1,128)} %gain_input.1, s32[8]{0:T(128)} %counts.1, s32[8]{0:T(128)} %dests.1, ...), custom_call_target="tpu_custom_call" | custom-call | tf_op jit(solution)/shard_map/pallas_call | solution.py:685
  111.5 0.0 copy-start
  111.5 1.9 %copy.13 = bf16[1,256,896]{2,1,0:T(8,128)(2,1)} copy(bf16[1,256,896]{2,1,0:T(8,128)(2,1)} %bitcast.2) | data formatting | bytes 917504
  113.4 0.0 copy-done
  113.4 0.6 copy.14
Async XLA Ops:
  111.5 1.9 %copy-start = (bf16[64,896]{1,0:T(8,128)(2,1)S(1)}, bf16[64,896]{1,0:T(8,128)(2,1)}, u32[]{:S(2)}) copy-start(bf16[64,896]{1,0:T(8,128)(2,1)} %get-tuple-element.9) | copy-start | bytes 344068

commit v6 on v5

--- a/solution.py
+++ b/solution.py
@@ -513,11 +513,12 @@
                 preferred_element_type=F32,
             )
         out[rows_of(micro)] = total.astype(BF16)
-        store(micro).start()
 
         @pl.when(section < SECTIONS - 1)
         def _():
             relay(micro).start()
+
+        store(micro).start()
 
     def mix_some(half):
         for source in range(PLACERS, SECTIONS):

time: 114 us -> 114 us (level)
  no operation moved by 1% of the time
where the time goes in v6:
time: 114 us
  Pallas kernels  111 us (97%)
  local copies, waits for them, and re-layouts  2.51 us (2%)
    pallas_call x1, Pallas kernels, on_device(): pl.pallas_call(whole_kernel, out_shape=(jax.ShapeDtypeStruct((rows, width...  111 us
    unnamed x4, local copies, waits for them, and re-layouts  2.51 us

profile of v6, /device:TPU:6, one launch (start us, length us, event | category | flops | bytes accessed | tf_op | source)
XLA Modules:
  0.0 114.0 jit_solution(2492568323815153829)
XLA Ops:
  0.6 110.9 %shard_map.104 = (bf16[256,896]{1,0:T(8,128)(2,1)}, bf16[64,896]{1,0:T(8,128)(2,1)}) custom-call(bf16[256,896]{1,0:T(8,128)(2,1)} %text.1, bf16[64,2048]{1,0:T(8,128)(2,1)} %vision.1, bf16[64,896]{1,0:T(8,128)(2,1)} %proj.1, bf16[112,896]{1,0:T(8,128)(2,1)} %bitcast.3, f32[1,896]{1,0:T(1,128)} %gain_input.1, s32[8]{0:T(128)} %counts.1, s32[8]{0:T(128)} %dests.1, ...), custom_call_target="tpu_custom_call" | custom-call | tf_op jit(solution)/shard_map/pallas_call | solution.py:686
  111.5 0.0 copy-start
  111.5 1.9 %copy.13 = bf16[1,256,896]{2,1,0:T(8,128)(2,1)} copy(bf16[1,256,896]{2,1,0:T(8,128)(2,1)} %bitcast.2) | data formatting | bytes 917504
  113.4 0.0 copy-done
  113.4 0.6 copy.14
Async XLA Ops:
  111.5 1.9 %copy-start = (bf16[64,896]{1,0:T(8,128)(2,1)S(1)}, bf16[64,896]{1,0:T(8,128)(2,1)}, u32[]{:S(2)}) copy-start(bf16[64,896]{1,0:T(8,128)(2,1)} %get-tuple-element.9) | copy-start | bytes 344068
